TPU v7x, 512 devices: a whole 4x4x16 slice. The times are simulated.
512 devices in a mesh: branch: 8 (over z_lo), shard: 64 (over x, y, z_hi, core).
Axes of the slice: x: 4, y: 4, z: 16 (z_hi: 2, z_lo: 8; z = z_hi * 8 + z_lo), core: 2. Of those that a mesh axis runs over, the one named last changes fastest.
Arguments:
- key_weights: bfloat16 [8, 8192, 512], P('branch', 'shard'), may hold values from -3 to 3
- first_moment: float32 [8, 8192, 512], P('branch', 'shard'), may hold values from -6 to 6
- second_moment: float32 [8, 8192, 512], P('branch', 'shard'), may hold values from 0.01 to 4
- tokens: bfloat16 [1024, 8192], P('branch', 'shard'), may hold values from -6 to 6
- routes: int32 [1024, 2], P('branch'), may hold values from 0 to 7, all different within a row; in each aligned block of 128 rows (0 to 127, 128 to 255, ...) at most 64 rows name the same one
- route_weights: float32 [1024, 2], P('branch'), may hold values from 0.2 to 1
- gate_up: bfloat16 [8, 2, 4096, 8192], P('branch', None, 'shard'), may hold values from -0.0625 to 0.0625
- down_proj: bfloat16 [8, 4096, 8192], P('branch', None, 'shard'), may hold values from -0.09375 to 0.09375
Outputs:
- merged_key: bfloat16 [8192, 512], P('shard')
- merged_first: float32 [8192, 512], P('shard')
- merged_second: float32 [8192, 512], P('shard')
- mixed: bfloat16 [1024, 8192], P('branch', 'shard')
Inputs may be any that keep to these rules, and one draw needn't show every extreme that they name: `routes`: the two experts of a token differ. Among the 128 tokens of one branch group no expert is named by more than 64 tokens, a bound that some block reaches.
All inputs are finite; a program needn't handle non-finite values.
Results may differ from a plain program's by a relative error of at most 0.0058.
Values may be sent and summed in bfloat16 or wider, within the bound.
No kernel may reach another device: no remote copies, remote signals or barrier semaphores. Data moves between devices by JAX's collectives and lax.ppermute only.
A program may use at most 64 MiB of HBM per device.

v0:
```python
import jax
import jax.numpy as jnp
from jax import lax
from jax.sharding import PartitionSpec as P


def body(
    key_weights, first_moment, second_moment, tokens, routes, route_weights, gate_up, down_proj
):
    branches = lax.axis_size("branch")
    summed = lax.psum(
        (key_weights[0].astype(jnp.float32), first_moment[0], second_moment[0]), "branch"
    )
    merged_key = (summed[0] / branches).astype(jnp.bfloat16)
    merged_first = summed[1] / branches
    merged_second = summed[2] / branches
    group_rows = tokens.shape[0]
    width_here = tokens.shape[1]
    capacity = min(group_rows, 4 * group_rows // branches)
    slot_count = branches * capacity
    labels = jnp.arange(branches, dtype=jnp.int32)
    onehot = (routes[:, :, None] == labels).astype(jnp.int32)
    named = jnp.sum(onehot, axis=1)
    before = jnp.cumsum(named, axis=0) - named
    position = jnp.sum(onehot * before[:, None, :], axis=-1)
    slot = routes * capacity + position
    match = slot[:, :, None] == jnp.arange(slot_count, dtype=jnp.int32)
    filled = jnp.any(match, axis=(0, 1))
    token_ids = jnp.arange(group_rows, dtype=jnp.int32)
    owner = jnp.sum(jnp.where(match, token_ids[:, None, None], 0), axis=(0, 1))
    weights_here = gate_up[0]
    slotted = jnp.where(filled[:, None], tokens[owner], jnp.zeros((), jnp.bfloat16))
    arrived = lax.all_to_all(
        slotted.reshape(branches, capacity, width_here),
        "branch",
        split_axis=0,
        concat_axis=0,
        tiled=True,
    )
    expert_rows = arrived.reshape(slot_count, width_here)
    gated = jnp.einsum(
        "rn,gfn->grf",
        lax.all_gather(expert_rows, "shard", axis=1, tiled=True),
        weights_here,
        preferred_element_type=jnp.float32,
    )
    hidden = (jax.nn.silu(gated[0]) * gated[1]).astype(jnp.bfloat16)
    lower = down_proj[0]
    expert_out = jnp.dot(
        lax.all_gather(hidden, "shard", axis=1, tiled=True),
        lower,
        preferred_element_type=jnp.float32,
    )
    expert_out = expert_out.astype(jnp.bfloat16).reshape(branches, capacity, width_here)
    back = lax.all_to_all(expert_out, "branch", split_axis=0, concat_axis=0, tiled=True).reshape(
        slot_count, width_here
    )
    picked = back[slot].astype(jnp.float32)
    mixed = route_weights[:, 0:1] * picked[:, 0] + route_weights[:, 1:2] * picked[:, 1]
    return (merged_key, merged_first, merged_second, mixed.astype(jnp.bfloat16))


def solution(mesh):
    return jax.shard_map(
        body,
        mesh=mesh,
        in_specs=(
            P("branch", "shard", None),
            P("branch", "shard", None),
            P("branch", "shard", None),
            P("branch", "shard"),
            P("branch", None),
            P("branch", None),
            P("branch", None, "shard", None),
            P("branch", None, "shard"),
        ),
        out_specs=(P("shard", None), P("shard", None), P("shard", None), P("branch", "shard")),
        check_vma=False,
    )
```

profile of v0, /device:TPU:6, one launch (start us, length us, event | category | flops | bytes accessed | tf_op | source)
XLA Modules:
  0.0 417.0 jit_solution(13937083683947777556)
XLA Ops:
  8.0 0.0 copy-start
  8.0 0.0 all-gather.3.cloned.1.call-start
  8.1 0.8 convert_reduce_fusion
  8.9 0.1 copy.21
  9.0 0.2 reduce_window_sum.11
  9.2 0.7 select_reduce_fusion.1
  9.9 0.7 compare_select_fusion.1
  10.6 0.1 select_reduce_fusion
  10.8 0.2 fusion.9
  10.9 0.1 broadcast_in_dim.37
  11.0 1.8 gather_fusion
  12.8 0.1 broadcast_select_fusion
  13.0 24.4 %all_to_all.10 = bf16[8,64,128]{2,1,0:T(8,128)(2,1)} all-to-all(bf16[8,64,128]{2,1,0:T(8,128)(2,1)S(1)} %broadcast_select_fusion), channel_id=1, replica_groups=mesh['branch'=8,'shard'=64] {'branch'}, dimensions={0} | all-to-all | bytes 262144 | tf_op jit(solution)/shard_map/all_to_all | solution.py:33
  37.4 0.0 all-gather.3.cloned.1.call-update
  37.4 0.0 copy-start.1
  37.4 0.0 copy-start.2
  37.4 0.0 copy-start.3
  37.4 0.0 all-gather.5.cloned.1.call-start
  37.5 209.7 %all-gather.3.cloned.1.call-done = bf16[512,8192]{1,0:T(8,128)(2,1)} async-done(((bf16[512,128]{1,0:T(8,128)(2,1)}), bf16[512,8192]{1,0:T(8,128)(2,1)}) %all-gather.3.cloned.1.call-update) | async-done | bytes 8388624 | tf_op jit(solution)/shard_map/all_gather | solution.py:43
  247.2 0.0 copy-done
  247.2 6.3 %fusion.3 = f32[2,512,64]{1,2,0:T(8,128)S(1)} fusion(bf16[1,2,64,8192]{3,2,1,0:T(8,128)(2,1)S(1)} %copy-done, bf16[512,8192]{1,0:T(8,128)(2,1)} %all-gather.3.cloned.1.call-done), kind=kOutput, calls=%fused_computation.5 | convolution fusion | flops 1073741824 | bytes 10747904 | tf_op jit(solution)/shard_map/rn,gfn->grf/dot_general | solution.py:41
  253.5 0.7 fusion.11
  254.2 0.0 all-gather.5.cloned.1.call-update
  254.2 0.0 all-reduce.3.cloned.1.call-start
  254.2 0.0 copy-done.1
  254.2 0.7 bitcast_convert_fusion
  255.0 0.0 all-reduce.3.cloned.1.call-update
  255.0 0.1 copy.24
  255.1 0.1 reshape.65
  255.3 0.0 copy-done.2
  255.3 114.7 %all-gather.5.cloned.1.call-done = bf16[512,4096]{0,1:T(8,128)(2,1)} async-done(((bf16[512,64]{0,1:T(8,128)(2,1)}), bf16[512,4096]{0,1:T(8,128)(2,1)}) %all-gather.5.cloned.1.call-update) | async-done | bytes 4194320 | tf_op jit(solution)/shard_map/all_gather | solution.py:50
  370.0 0.0 copy-done.3
  370.0 4.2 convolution_convert_fusion
  374.1 12.2 %all-to-all-start.1 = ((bf16[8,64,128]{2,1,0:T(8,128)(2,1)}), bf16[8,64,128]{2,1,0:T(8,128)(2,1)S(1)}, u32[]{:S(2)}, u32[]{:S(2)}) async-start(bf16[8,64,128]{2,1,0:T(8,128)(2,1)} %bitcast.14), calls=%async_computation.1 | async-start | bytes 262144 | tf_op jit(solution)/shard_map/all_to_all | solution.py:55
  386.3 18.1 %all-reduce.3.cloned.1.call-done = (f32[128,512]{1,0:T(8,128)}, f32[128,512]{1,0:T(8,128)}, f32[128,512]{1,0:T(8,128)}) async-done(((f32[128,512]{1,0:T(8,128)}, f32[128,512]{1,0:T(8,128)}, f32[128,512]{1,0:T(8,128)}), (f32[128,512]{1,0:T(8,128)}, f32[128,512]{1,0:T(8,128)}, f32[128,512]{1,0:T(8,128)})) %all-reduce.3.cloned.1.call-update) | async-done | bytes 786448 | tf_op jit(solution)/shard_map/psum | solution.py:11
  404.4 1.7 broadcast_multiply_fusion.1
  406.1 1.8 multiply_convert_fusion
  407.9 0.0 all-to-all-done.1
  407.9 0.9 gather_fusion.1
  408.8 0.1 fusion.12
  408.9 0.7 add_convert_fusion
  (6 shorter events, 0.1 us)
Async XLA Ops:
  8.0 239.2 %copy-start = (bf16[1,2,64,8192]{3,2,1,0:T(8,128)(2,1)S(1)}, bf16[1,2,64,8192]{3,2,1,0:T(8,128)(2,1)}, u32[]{:S(2)}) copy-start(bf16[1,2,64,8192]{3,2,1,0:T(8,128)(2,1)} %param.14) | copy-start | bytes 6291460
  8.0 239.2 %all-gather.3.cloned.1.call-start = ((), (), s32[]{:S(2)}) async-start(), calls=%async_computation.2 | async-start | bytes 8519680 | tf_op jit(solution)/shard_map/all_gather | solution.py:43
  37.4 216.8 %copy-start.1 = (bf16[1,128,512]{2,1,0:T(8,128)(2,1)S(1)}, bf16[1,128,512]{2,1,0:T(8,128)(2,1)}, u32[]{:S(2)}) copy-start(bf16[1,128,512]{2,1,0:T(8,128)(2,1)} %param.8) | copy-start | bytes 393220
  37.4 217.9 %copy-start.2 = (f32[128,2]{0,1:T(2,128)S(1)}, f32[128,2]{0,1:T(2,128)}, u32[]{:S(2)}) copy-start(f32[128,2]{0,1:T(2,128)} %param.13) | copy-start | bytes 3076
  37.4 332.6 %copy-start.3 = (bf16[1,4096,128]{2,1,0:T(8,128)(2,1)S(1)}, bf16[1,4096,128]{2,1,0:T(8,128)(2,1)}, u32[]{:S(2)}) copy-start(bf16[1,4096,128]{2,1,0:T(8,128)(2,1)} %param.15) | copy-start | bytes 3145732
  37.4 332.5 %all-gather.5.cloned.1.call-start = ((), (), s32[]{:S(2)}) async-start(), calls=%async_computation.3 | async-start | bytes 4259840 | tf_op jit(solution)/shard_map/all_gather | solution.py:50
  254.2 150.2 %all-reduce.3.cloned.1.call-start = ((), (), s32[]{:S(2)}) async-start(), calls=%async_computation.4 | async-start | bytes 1572864 | tf_op jit(solution)/shard_map/psum | solution.py:11
  374.1 33.8 %all-to-all-start.1 = ((bf16[8,64,128]{2,1,0:T(8,128)(2,1)}), bf16[8,64,128]{2,1,0:T(8,128)(2,1)S(1)}, u32[]{:S(2)}, u32[]{:S(2)}) async-start(bf16[8,64,128]{2,1,0:T(8,128)(2,1)} %bitcast.14), calls=%async_computation.1 | async-start | bytes 262144 | tf_op jit(solution)/shard_map/all_to_all | solution.py:55
Sparse Core Ops, SparseCore 0:
  37.5 209.6 all-gather.2
  254.3 115.6 all-gather.4
Sparse Core Ops, SparseCore 1:
  258.4 146.0 all-reduce.2
where the time goes:
time: 417 us
  waiting for transfers between devices  343 us (82%)
  blocking collectives  24.4 us (6%)
  between operations  15.6 us (4%)
  starting transfers between devices  12.3 us (3%)
  matrix products  10.4 us (2%)
  other arithmetic  8.45 us (2%)
    all_gather x1, waiting for transfers between devices, body(): lax.all_gather(expert_rows, 'shard', axis=1, tiled=True)  210 us
    all_gather x1, waiting for transfers between devices, body(): lax.all_gather(hidden, 'shard', axis=1, tiled=True)  115 us
    all_to_all x1, blocking collectives, body(): lax.all_to_all(slotted.reshape(branches, capacity, width_here), 'branch',...  24.4 us
    psum x1, waiting for transfers between devices, body(): lax.psum((key_weights[0].astype(jnp.float32), first_moment[0], second_mom...  18.1 us
    all_to_all x1, starting transfers between devices, body(): lax.all_to_all(expert_out, 'branch', split_axis=0, concat_axis=0, tiled=T...  12.2 us
  transfers between devices with their start and end apart: 4, of which 3 were waited for; matrix products, arithmetic and copies ran while one was open for 2% of the time, Pallas kernels for 0%

commit v1 on v0

v1 whole, which is shorter than its diff:
```python
import jax
import jax.numpy as jnp
from jax import lax
from jax.experimental import pallas as pl
from jax.experimental.pallas import tpu as pltpu
from jax.sharding import Mesh
from jax.sharding import PartitionSpec as P

SIDE = 4
GATE_ORDER, DOWN_ORDER = (0, 1, 3, 2), (0, 2, 1, 3)
VMEM = 48 * 1024 * 1024
BF16, F32 = jnp.bfloat16, jnp.float32
SHARD = ("x", "y", "zh", "c")


def shift(array, axis, step):
    size = lax.axis_size(axis)
    return lax.ppermute(array, axis, [(i, (i + step) % size) for i in range(size)])


def flip(array, axis, bit=1):
    return lax.ppermute(array, axis, [(i, i ^ bit) for i in range(lax.axis_size(axis))])


def exchange(blocks, axis):
    return lax.all_to_all(blocks, axis, split_axis=0, concat_axis=0, tiled=True)


def gather(block, axis):
    size = lax.axis_size(axis)
    return exchange(jnp.broadcast_to(block[None], (size,) + block.shape), axis)


def to_peers(cuts, order):
    return [shift(cuts[step], "x", step) if step else cuts[step] for step in order]


def call(kernel, out_shape, at, *arrays):
    many = isinstance(out_shape, (list, tuple))
    vmem = pl.BlockSpec(memory_space=pltpu.VMEM)
    return pl.pallas_call(
        kernel,
        out_shape=out_shape,
        in_specs=[pl.BlockSpec(memory_space=pltpu.SMEM)] + [vmem] * len(arrays),
        out_specs=[vmem] * len(out_shape) if many else vmem,
        compiler_params=pltpu.CompilerParams(vmem_limit_bytes=VMEM),
    )(at, *arrays)


def route_kernel(at_ref, routes_ref, tokens_ref, slotted_ref, pick_ref):
    rows = tokens_ref.shape[0]
    slots = slotted_ref.shape[0] // 2
    experts = 8
    capacity = slots // experts
    label = lax.broadcasted_iota(jnp.int32, (experts, rows), 0)
    first = (routes_ref[0:1, :] == label).astype(F32)
    second = (routes_ref[1:2, :] == label).astype(F32)
    named = first + second
    earlier = (
        lax.broadcasted_iota(jnp.int32, (rows, rows), 0)
        < lax.broadcasted_iota(jnp.int32, (rows, rows), 1)
    ).astype(F32)
    before = jnp.dot(named, earlier, preferred_element_type=F32).astype(jnp.int32)
    position = lax.broadcasted_iota(jnp.int32, (capacity, rows), 0)
    members = []
    for e in range(experts):
        hit = (before[e : e + 1] == position).astype(F32)
        span = slice(e * capacity, (e + 1) * capacity)
        pick_ref[span, :rows] = (hit * first[e : e + 1]).astype(BF16)
        pick_ref[span, rows:] = (hit * second[e : e + 1]).astype(BF16)
        members.append((hit * named[e : e + 1]).astype(BF16))
    slotted = jnp.dot(
        jnp.concatenate(members, axis=0), tokens_ref[...], preferred_element_type=F32
    ).astype(BF16)
    slotted_ref[:slots] = slotted
    slotted_ref[slots:] = slotted


def split_kernel(at_ref, gate_ref, *out_refs):
    wide, cols = gate_ref.shape[1] // SIDE, gate_ref.shape[0]
    for step, out_ref in enumerate(out_refs):
        x = lax.rem(at_ref[0] + step, SIDE)
        for j in range(wide // 128):
            lanes = pl.ds(pl.multiple_of(x * wide + j * 128, 128), 128)
            out_ref[j * cols : (j + 1) * cols, :] = gate_ref[:, lanes]


def gate_kernel(at_ref, w0, w1, w2, w3, own_ref, other_ref, here_ref, out_ref):
    rows = jnp.concatenate(
        [ref[y] for ref in (own_ref, other_ref) for y in range(SIDE)], axis=1
    )
    for step, w_ref in zip(GATE_ORDER, (w0, w1, w2, w3)):
        x = lax.rem(at_ref[0] + SIDE - step, SIDE)
        parts = []
        for core in (at_ref[2], 1 - at_ref[2]):
            for ahead in range(SIDE):
                chip = lax.rem(at_ref[1] + ahead, SIDE) * 2
                for half in range(2):
                    j = (chip + half) * 2 + core
                    parts.append(w_ref[pl.ds(pl.multiple_of(j * 128, 128), 128), :])
        total = lax.dot_general(
            jnp.concatenate(parts, axis=1),
            rows,
            (((1,), (1,)), ((), ())),
            preferred_element_type=F32,
        )
        out_ref[x] = total.astype(BF16)
        if step == 0:
            here_ref[...] = total


def down_kernel(at_ref, w0, w1, w2, w3, own_ref, other_ref, here_ref, out_ref):
    hidden = jnp.concatenate(
        [ref[y] for ref in (own_ref, other_ref) for y in range(SIDE)], axis=0
    )
    deep = own_ref.shape[1] // 2
    for step, w_ref in zip(DOWN_ORDER, (w0, w1, w2, w3)):
        x = lax.rem(at_ref[0] + SIDE - step, SIDE)
        parts = [
            w_ref[pl.ds(pl.multiple_of((chip * 2 + core) * deep, deep), deep), :]
            for core in (at_ref[2], 1 - at_ref[2])
            for chip in range(2 * SIDE)
        ]
        total = lax.dot_general(
            hidden,
            jnp.concatenate(parts, axis=0),
            (((0,), (0,)), ((), ())),
            preferred_element_type=F32,
        )
        out_ref[x] = total.astype(BF16)
        if step == 0:
            here_ref[...] = total


def partial_sums(kernel, shape, at, *arrays):
    shapes = [jax.ShapeDtypeStruct(shape, F32), jax.ShapeDtypeStruct((SIDE,) + shape, BF16)]
    return call(kernel, shapes, at, *arrays)


def add_back(here, got, x):
    for step in range(SIDE):
        here = here + jnp.where(x == step, 0.0, got[step].astype(F32))
    return here


def body(
    key_weights, first_moment, second_moment, tokens, routes, route_weights, gate_up, down_proj
):
    branches = lax.axis_size("b")
    half, x = lax.axis_index("zh"), lax.axis_index("x")
    at = jnp.stack([x, lax.axis_index("y"), lax.axis_index("c")]).astype(jnp.int32)
    branch = lax.axis_index("b")
    group_rows, width = tokens.shape
    capacity = 4 * group_rows // branches
    slots = branches * capacity
    hidden_here = gate_up.shape[2]
    rows_here = key_weights.shape[1]

    slotted, pick = call(
        route_kernel,
        [
            jax.ShapeDtypeStruct((2 * slots, width), BF16),
            jax.ShapeDtypeStruct((slots, 2 * group_rows), BF16),
        ],
        at,
        routes.T,
        tokens,
    )
    arrived = exchange(slotted.reshape(2 * branches, capacity, width), ("zh", "b"))

    gate_w = gate_up[0].reshape(2 * hidden_here, -1)
    cuts = call(
        split_kernel,
        [jax.ShapeDtypeStruct((gate_w.size // SIDE // width, width), BF16)] * SIDE,
        at,
        gate_w,
    )

    slabs = jnp.concatenate(
        [key_weights[0], first_moment[0].astype(BF16), second_moment[0].astype(BF16)], axis=0
    )
    slabs = slabs.reshape(2, 2, -1, slabs.shape[1])
    low, mid = branch % 2, (branch // 2) % 2
    give = lax.dynamic_index_in_dim(slabs, 1 - low, 0, keepdims=False)
    keep = lax.dynamic_index_in_dim(slabs, low, 0, keepdims=False)
    cuts, give = lax.optimization_barrier((cuts, give))
    weights = to_peers(cuts, GATE_ORDER)
    got = flip(give, "b", 1)
    arrived, got = lax.optimization_barrier((arrived, got))

    arrived = arrived.reshape(2, slots, width)
    rows = jnp.concatenate([arrived[0], arrived[1]], axis=1)
    line = [rows] + [shift(rows, "y", -ahead) for ahead in (1, 2, 3)]
    line, weights = lax.optimization_barrier((line, weights))
    line = jnp.stack(line)
    line_other = flip(line, "c")

    slabs = keep.astype(F32) + got.astype(F32)
    give = lax.dynamic_index_in_dim(slabs, 1 - mid, 0, keepdims=False).astype(BF16)
    keep = lax.dynamic_index_in_dim(slabs, mid, 0, keepdims=False)
    got = flip(give, "b", 2)

    here, others = partial_sums(
        gate_kernel,
        (2 * hidden_here, slots),
        at,
        *weights,
        line,
        line_other,
    )
    others, got = lax.optimization_barrier((others, got))
    slabs = (keep.astype(BF16).astype(F32) + got.astype(F32)).astype(BF16)
    got = flip(slabs, "b", 4)
    gated = add_back(here, exchange(others, "x"), x)
    hidden = (jax.nn.silu(gated[:hidden_here]) * gated[hidden_here:]).astype(BF16)

    swap = flip(hidden, "zh")
    lower = down_proj[0].reshape(SIDE, -1, width)
    cuts = [lower[lax.rem(x + step, SIDE)] for step in range(SIDE)]
    cuts, hidden = lax.optimization_barrier((cuts, hidden))
    weights = to_peers(cuts, DOWN_ORDER)
    swap, got = lax.optimization_barrier((swap, got))
    slabs = ((slabs.astype(F32) + got.astype(F32)) / branches).astype(BF16)
    got = flip(slabs, "b", 2)
    both = jnp.where(
        half == 0,
        jnp.concatenate([hidden, swap], axis=0),
        jnp.concatenate([swap, hidden], axis=0),
    )
    line = gather(both, "y")
    line, weights, got = lax.optimization_barrier((line, weights, got))
    slabs = jnp.stack([jnp.where(mid == 0, slabs, got), jnp.where(mid == 0, got, slabs)])
    got = flip(slabs, "b", 1)
    here, others = partial_sums(
        down_kernel, (slots, width), at, *weights, line, flip(line, "c")
    )
    others, got = lax.optimization_barrier((others, got))
    out = add_back(here, exchange(others, "x"), x).astype(BF16)
    out, slabs, got = lax.optimization_barrier((out, slabs, got))

    back = exchange(out.reshape(branches, capacity, width), "b").reshape(slots, width)
    slabs = jnp.stack([jnp.where(low == 0, slabs, got), jnp.where(low == 0, got, slabs)])
    slabs = slabs.reshape(3 * rows_here, -1)
    picked = lax.dot_general(
        pick, back, (((0,), (0,)), ((), ())), preferred_element_type=F32
    )
    mixed = (
        route_weights[:, 0:1] * picked[:group_rows] + route_weights[:, 1:2] * picked[group_rows:]
    ).astype(BF16)
    return (
        slabs[:rows_here],
        slabs[rows_here : 2 * rows_here].astype(F32),
        slabs[2 * rows_here :].astype(F32),
        mixed,
    )


def solution(mesh):
    fine = Mesh(mesh.devices.reshape(8, SIDE, SIDE, 2, 2), ("b",) + SHARD)
    return jax.shard_map(
        body,
        mesh=fine,
        in_specs=(
            P("b", SHARD, None),
            P("b", SHARD, None),
            P("b", SHARD, None),
            P("b", SHARD),
            P("b", None),
            P("b", None),
            P("b", None, SHARD, None),
            P("b", None, SHARD),
        ),
        out_specs=(P(SHARD, None), P(SHARD, None), P(SHARD, None), P("b", SHARD)),
        check_vma=False,
    )
```

time: 417 us -> 175 us (0.42)
  waiting for transfers between devices: 343 us -> 41.1 us
  starting transfers between devices: 12.3 us -> 103 us
  blocking collectives: 24.4 us -> 0 us
  between operations: 15.6 us -> 1.12 us
  matrix products: 10.4 us -> 0.27 us
  Pallas kernels: 0 us -> 9.39 us
  local copies, waits for them, and re-layouts: 3.28 us -> 10.9 us
    all_gather x2 -> x0, waiting for transfers between devices: 324 us -> none  [the longest x1 210 us: body(): lax.all_gather(expert_rows, 'shard', axis=1, tiled=True)]
    ppermute x0 -> x17, starting transfers between devices: none -> 67.3 us  [the longest x8 38.3 us: flip(): lax.ppermute(array, axis, [(i, i ^ bit) for i in range(lax.axis_size(axis...]
    all_to_all x1 -> x0, blocking collectives: 24.4 us -> none  [body(): lax.all_to_all(slotted.reshape(branches, capacity, width_here), 'branch',...]
    all_to_all x1 -> x5, starting transfers between devices: 12.2 us -> 35.7 us  [exchange(): return lax.all_to_all(blocks, axis, split_axis=0, concat_axis=0, tiled=True)]
    ppermute x0 -> x17, waiting for transfers between devices: none -> 22.2 us  [the longest x8 13.8 us: flip(): lax.ppermute(array, axis, [(i, i ^ bit) for i in range(lax.axis_size(axis...]
    all_to_all x1 -> x5, waiting for transfers between devices: 0.01 us -> 18.9 us  [exchange(): return lax.all_to_all(blocks, axis, split_axis=0, concat_axis=0, tiled=True)]
    psum x1 -> x0, waiting for transfers between devices: 18.1 us -> none  [body(): lax.psum((key_weights[0].astype(jnp.float32), first_moment[0], second_mom...]
    dot_general x2 -> x1, matrix products: 10.4 us -> 0.27 us  [body(): lax.dot_general(pick, back, (((0,), (0,)), ((), ())), preferred_element_t...]
  transfers between devices with their start and end apart: 4 -> 22, of which waited for: 3 -> 9; matrix products, arithmetic and copies ran while one was open for 2% -> 3% of each run, Pallas kernels for 0% -> 5%
where the time goes in v1:
time: 175 us; the launch traced here: 172 us
  starting transfers between devices  103 us (59%)
  waiting for transfers between devices  41.1 us (23%)
  local copies, waits for them, and re-layouts  10.9 us (6%)
  Pallas kernels  9.39 us (5%)
  other arithmetic  5.93 us (3%)
    ppermute x8, starting transfers between devices, flip(): lax.ppermute(array, axis, [(i, i ^ bit) for i in range(lax.axis_size(axis...  38.3 us
    all_to_all x5, starting transfers between devices, exchange(): return lax.all_to_all(blocks, axis, split_axis=0, concat_axis=0, tiled=True)  35.7 us
    ppermute x9, starting transfers between devices, shift(): lax.ppermute(array, axis, [(i, (i + step) % size) for i in range(size)])  29 us
    all_to_all x5, waiting for transfers between devices, exchange(): return lax.all_to_all(blocks, axis, split_axis=0, concat_axis=0, tiled=True)  18.9 us
    ppermute x8, waiting for transfers between devices, flip(): lax.ppermute(array, axis, [(i, i ^ bit) for i in range(lax.axis_size(axis...  13.8 us
    pallas_call x4, Pallas kernels, call(): pl.pallas_call(kernel, out_shape=out_shape, in_specs=[pl.BlockSpec(memory...  9.39 us
    unnamed x32, local copies, waits for them, and re-layouts  8.92 us
    ppermute x9, waiting for transfers between devices, shift(): lax.ppermute(array, axis, [(i, (i + step) % size) for i in range(size)])  8.43 us
  transfers between devices with their start and end apart: 22, of which 9 were waited for; matrix products, arithmetic and copies ran while one was open for 3% of the time, Pallas kernels for 5%

profile of v1, /device:TPU:6, one launch (start us, length us, event | category | flops | bytes accessed | tf_op | source)
XLA Modules:
  0.0 171.7 jit_solution(5323486118993819476)
XLA Ops:
  0.6 0.1 pad_add_fusion.at_ref
  0.7 0.8 copy-done.7
  1.5 0.7 copy-done.8
  2.2 1.6 shard_map.111
  3.7 15.2 %all-to-all-start = ((bf16[16,64,128]{2,1,0:T(8,128)(2,1)}), bf16[16,64,128]{2,1,0:T(8,128)(2,1)}, u32[]{:S(2)}, u32[]{:S(2)}) async-start(bf16[16,64,128]{2,1,0:T(8,128)(2,1)} %bitcast.9), calls=%async_computation | async-start | bytes 524288 | tf_op jit(solution)/shard_map/all_to_all | solution.py:26
  19.0 0.0 copy-start
  19.0 1.6 copy-done
  20.6 1.9 %shard_map.112 = (bf16[2048,128]{1,0:T(8,128)(2,1)S(1)}, bf16[2048,128]{1,0:T(8,128)(2,1)}, bf16[2048,128]{1,0:T(8,128)(2,1)S(1)}, bf16[2048,128]{1,0:T(8,128)(2,1)S(1)}) custom-call(s32[3]{0:T(128)S(1)} %pad_add_fusion.at_ref, bf16[128,8192]{1,0:T(8,128)(2,1)S(1)} %bitcast.86), custom_call_target="tpu_custom_call" | custom-call | tf_op jit(solution)/shard_map/pallas_call | solution.py:41
  22.6 0.7 copy-done.9
  23.3 3.8 %collective-permute-start = (bf16[2,96,512]{2,1,0:T(8,128)(2,1)S(1)}, bf16[2,96,512]{2,1,0:T(8,128)(2,1)}, u32[]{:S(2)}, u32[]{:S(2)}) collective-permute-start(bf16[2,96,512]{2,1,0:T(8,128)(2,1)S(1)} %dynamic-slice_bitcast_fusion.4), channel_id=1, source_target_pairs={{0,64},{64,0},{128,192},{192,128},{256,320},{320,256},{384,448},{4... | collective-permute-start | bytes 589832 | tf_op jit(solution)/shard_map/ppermute | solution.py:22
  27.1 2.4 %collective-permute-start.4 = (bf16[2048,128]{1,0:T(8,128)(2,1)}, bf16[2048,128]{1,0:T(8,128)(2,1)S(1)}, u32[]{:S(2)}, u32[]{:S(2)}) collective-permute-start(bf16[2048,128]{1,0:T(8,128)(2,1)} %get-tuple-element.57), channel_id=1, source_target_pairs={{0,16},{16,32},{32,48},{48,0},{1,17},{17,33},{33,49},{49,1},{2,18}... | collective-permute-start | bytes 1572872 | tf_op jit(solution)/shard_map/ppermute | solution.py:18
  29.5 3.5 %collective-permute-start.5 = (bf16[2048,128]{1,0:T(8,128)(2,1)S(1)}, bf16[2048,128]{1,0:T(8,128)(2,1)S(1)}, u32[]{:S(2)}, u32[]{:S(2)}) collective-permute-start(bf16[2048,128]{1,0:T(8,128)(2,1)S(1)} %get-tuple-element.58), channel_id=1, source_target_pairs={{0,48},{16,0},{32,16},{48,32},{1,49},{17,1},{33,17},{49,33},{2,50}... | collective-permute-start | bytes 1572872 | tf_op jit(solution)/shard_map/ppermute | solution.py:18
  32.9 3.3 %collective-permute-start.6 = (bf16[2048,128]{1,0:T(8,128)(2,1)S(1)}, bf16[2048,128]{1,0:T(8,128)(2,1)S(1)}, u32[]{:S(2)}, u32[]{:S(2)}) collective-permute-start(bf16[2048,128]{1,0:T(8,128)(2,1)S(1)} %get-tuple-element.59), channel_id=1, source_target_pairs={{0,32},{16,48},{32,0},{48,16},{1,33},{17,49},{33,1},{49,17},{2,34}... | collective-permute-start | bytes 1572872 | tf_op jit(solution)/shard_map/ppermute | solution.py:18
  36.3 0.5 collective-permute-done
  36.8 0.6 all-to-all-done
  37.4 1.0 fusion.7
  38.4 4.9 %collective-permute-start.1 = (bf16[512,256]{1,0:T(8,128)(2,1)S(1)}, bf16[512,256]{1,0:T(8,128)(2,1)S(1)}, u32[]{:S(2)}, u32[]{:S(2)}) collective-permute-start(bf16[512,256]{1,0:T(8,128)(2,1)S(1)} %pad_maximum_fusion.3), channel_id=1, source_target_pairs={{0,12},{4,0},{8,4},{12,8},{1,13},{5,1},{9,5},{13,9},{2,14},{6,2},{... | collective-permute-start | bytes 786440 | tf_op jit(solution)/shard_map/ppermute | solution.py:18
  43.4 2.5 %collective-permute-start.2 = (bf16[512,256]{1,0:T(8,128)(2,1)S(1)}, bf16[512,256]{1,0:T(8,128)(2,1)S(1)}, u32[]{:S(2)}, u32[]{:S(2)}) collective-permute-start(bf16[512,256]{1,0:T(8,128)(2,1)S(1)} %pad_maximum_fusion.3), channel_id=1, source_target_pairs={{0,8},{4,12},{8,0},{12,4},{1,9},{5,13},{9,1},{13,5},{2,10},{6,14},... | collective-permute-start | bytes 786440 | tf_op jit(solution)/shard_map/ppermute | solution.py:18
  45.9 2.9 %collective-permute-start.3 = (bf16[512,256]{1,0:T(8,128)(2,1)S(1)}, bf16[512,256]{1,0:T(8,128)(2,1)S(1)}, u32[]{:S(2)}, u32[]{:S(2)}) collective-permute-start(bf16[512,256]{1,0:T(8,128)(2,1)S(1)} %pad_maximum_fusion.3), channel_id=1, source_target_pairs={{0,4},{4,8},{8,12},{12,0},{1,5},{5,9},{9,13},{13,1},{2,6},{6,10},{... | collective-permute-start | bytes 786440 | tf_op jit(solution)/shard_map/ppermute | solution.py:18
  48.8 7.6 %collective-permute-done.5.w2 = bf16[2048,128]{1,0:T(8,128)(2,1)S(1)} collective-permute-done((bf16[2048,128]{1,0:T(8,128)(2,1)S(1)}, bf16[2048,128]{1,0:T(8,128)(2,1)S(1)}, u32[]{:S(2)}, u32[]{:S(2)}) %collective-permute-start.5) | collective-permute-done | bytes 524320 | tf_op jit(solution)/shard_map/ppermute | solution.py:18
  56.4 0.8 copy-done.1
  57.2 0.0 collective-permute-done.6.w3
  57.2 0.8 copy-done.3
  58.0 0.0 collective-permute-done.2
  58.0 0.9 collective-permute-done.3
  58.8 0.1 pad_maximum_fusion.own_ref
  59.0 1.9 %collective-permute-start.7 = (bf16[4,512,256]{2,1,0:T(8,128)(2,1)S(1)}, bf16[4,512,256]{2,1,0:T(8,128)(2,1)S(1)}, u32[]{:S(2)}, u32[]{:S(2)}) collective-permute-start(bf16[4,512,256]{2,1,0:T(8,128)(2,1)S(1)} %pad_maximum_fusion.own_ref), channel_id=1, source_target_pairs={{0,1},{1,0},{2,3},{3,2},{4,5},{5,4},{6,7},{7,6},{8,9},{9,8},{10,11... | collective-permute-start | bytes 3145736 | tf_op jit(solution)/shard_map/ppermute | solution.py:22
  60.9 1.1 convert_add_fusion
  62.0 0.0 copy-start.11
  62.0 5.0 %collective-permute-start.8 = (bf16[96,512]{1,0:T(8,128)(2,1)S(1)}, bf16[96,512]{1,0:T(8,128)(2,1)S(1)}, u32[]{:S(2)}, u32[]{:S(2)}) collective-permute-start(bf16[96,512]{1,0:T(8,128)(2,1)S(1)} %fusion.3), channel_id=1, source_target_pairs={{0,128},{64,192},{128,0},{192,64},{256,384},{320,448},{384,256},{4... | collective-permute-start | bytes 294920 | tf_op jit(solution)/shard_map/ppermute | solution.py:22
  67.1 1.0 copy-done.2
  68.1 1.0 copy-done.4
  69.1 3.3 %shard_map.113 = (f32[128,512]{1,0:T(8,128)S(1)}, bf16[4,128,512]{2,1,0:T(8,128)(2,1)S(1)}) custom-call(s32[3]{0:T(128)S(1)} %pad_add_fusion.at_ref, bf16[2048,128]{1,0:T(8,128)(2,1)S(1)} %get-tuple-element.60.w0, bf16[2048,128]{1,0:T(8,128)(2,1)S(1)} %collective-permute-done.4.w1, bf16[2048,128]{1,0:T(8,128)(2,1)S(1)} %copy-done.2, ...), custom_call_target="tpu_custom_call" | custom-call | tf_op jit(solution)/shard_map/pallas_call | solution.py:41
  72.5 0.8 copy-done.5
  73.3 0.7 copy-done.6
  74.0 0.0 collective-permute-done.8
  74.0 4.9 %all-to-all-start.1 = ((bf16[4,128,512]{2,1,0:T(8,128)(2,1)}), bf16[4,128,512]{2,1,0:T(8,128)(2,1)S(1)}, u32[]{:S(2)}, u32[]{:S(2)}) async-start(bf16[4,128,512]{2,1,0:T(8,128)(2,1)} %copy-done.5), calls=%async_computation.1 | async-start | bytes 1048576 | tf_op jit(solution)/shard_map/all_to_all | solution.py:26
  78.9 0.9 fusion.1
  79.8 7.1 %collective-permute-start.10 = (bf16[96,512]{1,0:T(8,128)(2,1)S(1)}, bf16[96,512]{1,0:T(8,128)(2,1)S(1)}, u32[]{:S(2)}, u32[]{:S(2)}) collective-permute-start(bf16[96,512]{1,0:T(8,128)(2,1)S(1)} %fusion.1), channel_id=1, source_target_pairs={{0,256},{64,320},{128,384},{192,448},{256,0},{320,64},{384,128},{4... | collective-permute-start | bytes 294920 | tf_op jit(solution)/shard_map/ppermute | solution.py:22
  87.0 1.1 bitcast_add_fusion.4
  88.1 9.1 %collective-permute-start.9 = (bf16[64,512]{1,0:T(8,128)(2,1)S(1)}, bf16[64,512]{1,0:T(8,128)(2,1)S(1)}, u32[]{:S(2)}, u32[]{:S(2)}) collective-permute-start(bf16[64,512]{1,0:T(8,128)(2,1)S(1)} %fusion.2), channel_id=1, source_target_pairs={{0,2},{2,0},{1,3},{3,1},{4,6},{6,4},{5,7},{7,5},{8,10},{10,8},{9,1... | collective-permute-start | bytes 196616 | tf_op jit(solution)/shard_map/ppermute | solution.py:22
  97.2 0.1 dynamic-slice_bitcast_fusion
  97.3 0.0 collective-permute-done.10
  97.3 5.9 %collective-permute-done.9 = bf16[64,512]{1,0:T(8,128)(2,1)S(1)} collective-permute-done((bf16[64,512]{1,0:T(8,128)(2,1)S(1)}, bf16[64,512]{1,0:T(8,128)(2,1)S(1)}, u32[]{:S(2)}, u32[]{:S(2)}) %collective-permute-start.9) | collective-permute-done | bytes 65568 | tf_op jit(solution)/shard_map/ppermute | solution.py:22
  103.2 0.8 broadcast_in_dim.21
  104.0 3.5 %all-to-all-start.2 = ((bf16[4,128,512]{2,1,0:T(8,128)(2,1)}), bf16[4,128,512]{2,1,0:T(8,128)(2,1)S(1)}, u32[]{:S(2)}, u32[]{:S(2)}) async-start(bf16[4,128,512]{2,1,0:T(8,128)(2,1)} %broadcast_in_dim.21), calls=%async_computation.2 | async-start | bytes 1048576 | tf_op jit(solution)/shard_map/all_to_all | solution.py:26
  107.5 0.0 copy-start.15
  107.5 3.7 %collective-permute-start.11 = (bf16[1024,128]{1,0:T(8,128)(2,1)S(1)}, bf16[1024,128]{1,0:T(8,128)(2,1)S(1)}, u32[]{:S(2)}, u32[]{:S(2)}) collective-permute-start(bf16[1024,128]{1,0:T(8,128)(2,1)S(1)} %get-tuple-element.76), channel_id=1, source_target_pairs={{0,32},{16,48},{32,0},{48,16},{1,33},{17,49},{33,1},{49,17},{2,34}... | collective-permute-start | bytes 786440 | tf_op jit(solution)/shard_map/ppermute | solution.py:18
  111.2 3.5 %collective-permute-start.12 = (bf16[1024,128]{1,0:T(8,128)(2,1)S(1)}, bf16[1024,128]{1,0:T(8,128)(2,1)S(1)}, u32[]{:S(2)}, u32[]{:S(2)}) collective-permute-start(bf16[1024,128]{1,0:T(8,128)(2,1)S(1)} %get-tuple-element.77), channel_id=1, source_target_pairs={{0,16},{16,32},{32,48},{48,0},{1,17},{17,33},{33,49},{49,1},{2,18}... | collective-permute-start | bytes 786440 | tf_op jit(solution)/shard_map/ppermute | solution.py:18
  114.7 2.4 %collective-permute-start.13 = (bf16[1024,128]{1,0:T(8,128)(2,1)S(1)}, bf16[1024,128]{1,0:T(8,128)(2,1)S(1)}, u32[]{:S(2)}, u32[]{:S(2)}) collective-permute-start(bf16[1024,128]{1,0:T(8,128)(2,1)S(1)} %get-tuple-element.78), channel_id=1, source_target_pairs={{0,48},{16,0},{32,16},{48,32},{1,49},{17,1},{33,17},{49,33},{2,50}... | collective-permute-start | bytes 786440 | tf_op jit(solution)/shard_map/ppermute | solution.py:18
  117.1 2.9 %collective-permute-start.14 = (bf16[96,512]{1,0:T(8,128)(2,1)S(1)}, bf16[96,512]{1,0:T(8,128)(2,1)S(1)}, u32[]{:S(2)}, u32[]{:S(2)}) collective-permute-start(bf16[96,512]{1,0:T(8,128)(2,1)S(1)} %multiply_convert_fusion), channel_id=1, source_target_pairs={{0,128},{64,192},{128,0},{192,64},{256,384},{320,448},{384,256},{4... | collective-permute-start | bytes 294920 | tf_op jit(solution)/shard_map/ppermute | solution.py:22
  120.0 4.5 %collective-permute-done.14 = bf16[96,512]{1,0:T(8,128)(2,1)S(1)} collective-permute-done((bf16[96,512]{1,0:T(8,128)(2,1)S(1)}, bf16[96,512]{1,0:T(8,128)(2,1)S(1)}, u32[]{:S(2)}, u32[]{:S(2)}) %collective-permute-start.14) | collective-permute-done | bytes 98336 | tf_op jit(solution)/shard_map/ppermute | solution.py:22
  124.6 1.9 %collective-permute-start.15 = (bf16[4,128,512]{2,1,0:T(8,128)(2,1)S(1)}, bf16[4,128,512]{2,1,0:T(8,128)(2,1)S(1)}, u32[]{:S(2)}, u32[]{:S(2)}) collective-permute-start(bf16[4,128,512]{2,1,0:T(8,128)(2,1)S(1)} %all-to-all-done.2.own_ref), channel_id=1, source_target_pairs={{0,1},{1,0},{2,3},{3,2},{4,5},{5,4},{6,7},{7,6},{8,9},{9,8},{10,11... | collective-permute-start | bytes 1572872 | tf_op jit(solution)/shard_map/ppermute | solution.py:22
  126.5 6.6 %collective-permute-start.16 = (bf16[2,96,512]{2,1,0:T(8,128)(2,1)S(1)}, bf16[2,96,512]{2,1,0:T(8,128)(2,1)S(1)}, u32[]{:S(2)}, u32[]{:S(2)}) collective-permute-start(bf16[2,96,512]{2,1,0:T(8,128)(2,1)S(1)} %pad_maximum_fusion.4), channel_id=1, source_target_pairs={{0,64},{64,0},{128,192},{192,128},{256,320},{320,256},{384,448},{4... | collective-permute-start | bytes 589832 | tf_op jit(solution)/shard_map/ppermute | solution.py:22
  133.1 2.6 %shard_map.114 = (f32[512,128]{1,0:T(8,128)S(1)}, bf16[4,512,128]{2,1,0:T(8,128)(2,1)}) custom-call(s32[3]{0:T(128)S(1)} %pad_add_fusion.at_ref, bf16[1024,128]{1,0:T(8,128)(2,1)S(1)} %get-tuple-element.80.w0, bf16[1024,128]{1,0:T(8,128)(2,1)S(1)} %collective-permute-done.11.w1, bf16[1024,128]{1,0:T(8,128)(2,1)S(1)} %collective-permute-done.12.w2, ...), custom_call_target="tpu_custom_call" | custom-call | tf_op jit(solution)/shard_map/pallas_call | solution.py:41
  135.8 2.9 %collective-permute-done.16 = bf16[2,96,512]{2,1,0:T(8,128)(2,1)S(1)} collective-permute-done((bf16[2,96,512]{2,1,0:T(8,128)(2,1)S(1)}, bf16[2,96,512]{2,1,0:T(8,128)(2,1)S(1)}, u32[]{:S(2)}, u32[]{:S(2)}) %collective-permute-start.16) | collective-permute-done | bytes 196640 | tf_op jit(solution)/shard_map/ppermute | solution.py:22
  138.7 6.6 %all-to-all-start.3 = ((bf16[4,512,128]{2,1,0:T(8,128)(2,1)}), bf16[4,512,128]{2,1,0:T(8,128)(2,1)S(1)}, u32[]{:S(2)}, u32[]{:S(2)}) async-start(bf16[4,512,128]{2,1,0:T(8,128)(2,1)} %get-tuple-element.88), calls=%async_computation.3 | async-start | bytes 1048576 | tf_op jit(solution)/shard_map/all_to_all | solution.py:26
  145.3 7.8 %all-to-all-done.3 = bf16[4,512,128]{2,1,0:T(8,128)(2,1)S(1)} async-done(((bf16[4,512,128]{2,1,0:T(8,128)(2,1)}), bf16[4,512,128]{2,1,0:T(8,128)(2,1)S(1)}, u32[]{:S(2)}, u32[]{:S(2)}) %all-to-all-start.3) | async-done | bytes 524320 | tf_op jit(solution)/shard_map/all_to_all | solution.py:26
  153.1 0.8 fusion
  153.8 5.4 %all-to-all-start.4 = ((bf16[8,64,128]{2,1,0:T(8,128)(2,1)}), bf16[8,64,128]{2,1,0:T(8,128)(2,1)S(1)}, u32[]{:S(2)}, u32[]{:S(2)}) async-start(bf16[8,64,128]{2,1,0:T(8,128)(2,1)} %bitcast.39), calls=%async_computation.4 | async-start | bytes 262144 | tf_op jit(solution)/shard_map/all_to_all | solution.py:26
  159.3 0.9 slice_convert_fusion
  160.2 10.5 %all-to-all-done.4 = bf16[8,64,128]{2,1,0:T(8,128)(2,1)S(1)} async-done(((bf16[8,64,128]{2,1,0:T(8,128)(2,1)}), bf16[8,64,128]{2,1,0:T(8,128)(2,1)S(1)}, u32[]{:S(2)}, u32[]{:S(2)}) %all-to-all-start.4) | async-done | bytes 131104 | tf_op jit(solution)/shard_map/all_to_all | solution.py:26
  170.7 0.3 fusion.8
  171.0 0.7 fusion.6
  (41 shorter events, 0.4 us)
Async XLA Ops:
  0.7 0.8 copy-start.7
  1.5 0.7 copy-start.8
  2.2 20.3 %copy-start.12 = (f32[1,128,512]{2,1,0:T(8,128)S(1)}, f32[1,128,512]{2,1,0:T(8,128)}, u32[]{:S(2)}) copy-start(f32[1,128,512]{2,1,0:T(8,128)} %param.10) | copy-start | bytes 786436
  2.2 20.3 %copy-start.13 = (f32[1,128,512]{2,1,0:T(8,128)S(1)}, f32[1,128,512]{2,1,0:T(8,128)}, u32[]{:S(2)}) copy-start(f32[1,128,512]{2,1,0:T(8,128)} %param.9) | copy-start | bytes 786436
  3.7 33.7 %all-to-all-start = ((bf16[16,64,128]{2,1,0:T(8,128)(2,1)}), bf16[16,64,128]{2,1,0:T(8,128)(2,1)}, u32[]{:S(2)}, u32[]{:S(2)}) async-start(bf16[16,64,128]{2,1,0:T(8,128)(2,1)} %bitcast.9), calls=%async_computation | async-start | bytes 524288 | tf_op jit(solution)/shard_map/all_to_all | solution.py:26
  19.0 1.6 copy-start
  20.6 1.9 %copy-start.14 = (bf16[1,128,512]{2,1,0:T(8,128)(2,1)S(1)}, bf16[1,128,512]{2,1,0:T(8,128)(2,1)}, u32[]{:S(2)}) copy-start(bf16[1,128,512]{2,1,0:T(8,128)(2,1)} %param.8) | copy-start | bytes 393220
  22.6 0.8 copy-start.9
  23.3 13.5 %collective-permute-start = (bf16[2,96,512]{2,1,0:T(8,128)(2,1)S(1)}, bf16[2,96,512]{2,1,0:T(8,128)(2,1)}, u32[]{:S(2)}, u32[]{:S(2)}) collective-permute-start(bf16[2,96,512]{2,1,0:T(8,128)(2,1)S(1)} %dynamic-slice_bitcast_fusion.4), channel_id=1, source_target_pairs={{0,64},{64,0},{128,192},{192,128},{256,320},{320,256},{384,448},{4... | collective-permute-start | bytes 589832 | tf_op jit(solution)/shard_map/ppermute | solution.py:22
  27.1 18.8 %collective-permute-start.4 = (bf16[2048,128]{1,0:T(8,128)(2,1)}, bf16[2048,128]{1,0:T(8,128)(2,1)S(1)}, u32[]{:S(2)}, u32[]{:S(2)}) collective-permute-start(bf16[2048,128]{1,0:T(8,128)(2,1)} %get-tuple-element.57), channel_id=1, source_target_pairs={{0,16},{16,32},{32,48},{48,0},{1,17},{17,33},{33,49},{49,1},{2,18}... | collective-permute-start | bytes 1572872 | tf_op jit(solution)/shard_map/ppermute | solution.py:18
  29.5 26.9 %collective-permute-start.5 = (bf16[2048,128]{1,0:T(8,128)(2,1)S(1)}, bf16[2048,128]{1,0:T(8,128)(2,1)S(1)}, u32[]{:S(2)}, u32[]{:S(2)}) collective-permute-start(bf16[2048,128]{1,0:T(8,128)(2,1)S(1)} %get-tuple-element.58), channel_id=1, source_target_pairs={{0,48},{16,0},{32,16},{48,32},{1,49},{17,1},{33,17},{49,33},{2,50}... | collective-permute-start | bytes 1572872 | tf_op jit(solution)/shard_map/ppermute | solution.py:18
  32.9 24.2 %collective-permute-start.6 = (bf16[2048,128]{1,0:T(8,128)(2,1)S(1)}, bf16[2048,128]{1,0:T(8,128)(2,1)S(1)}, u32[]{:S(2)}, u32[]{:S(2)}) collective-permute-start(bf16[2048,128]{1,0:T(8,128)(2,1)S(1)} %get-tuple-element.59), channel_id=1, source_target_pairs={{0,32},{16,48},{32,0},{48,16},{1,33},{17,49},{33,1},{49,17},{2,34}... | collective-permute-start | bytes 1572872 | tf_op jit(solution)/shard_map/ppermute | solution.py:18
  38.4 19.5 %collective-permute-start.1 = (bf16[512,256]{1,0:T(8,128)(2,1)S(1)}, bf16[512,256]{1,0:T(8,128)(2,1)S(1)}, u32[]{:S(2)}, u32[]{:S(2)}) collective-permute-start(bf16[512,256]{1,0:T(8,128)(2,1)S(1)} %pad_maximum_fusion.3), channel_id=1, source_target_pairs={{0,12},{4,0},{8,4},{12,8},{1,13},{5,1},{9,5},{13,9},{2,14},{6,2},{... | collective-permute-start | bytes 786440 | tf_op jit(solution)/shard_map/ppermute | solution.py:18
  43.4 14.6 %collective-permute-start.2 = (bf16[512,256]{1,0:T(8,128)(2,1)S(1)}, bf16[512,256]{1,0:T(8,128)(2,1)S(1)}, u32[]{:S(2)}, u32[]{:S(2)}) collective-permute-start(bf16[512,256]{1,0:T(8,128)(2,1)S(1)} %pad_maximum_fusion.3), channel_id=1, source_target_pairs={{0,8},{4,12},{8,0},{12,4},{1,9},{5,13},{9,1},{13,5},{2,10},{6,14},... | collective-permute-start | bytes 786440 | tf_op jit(solution)/shard_map/ppermute | solution.py:18
  45.9 12.9 %collective-permute-start.3 = (bf16[512,256]{1,0:T(8,128)(2,1)S(1)}, bf16[512,256]{1,0:T(8,128)(2,1)S(1)}, u32[]{:S(2)}, u32[]{:S(2)}) collective-permute-start(bf16[512,256]{1,0:T(8,128)(2,1)S(1)} %pad_maximum_fusion.3), channel_id=1, source_target_pairs={{0,4},{4,8},{8,12},{12,0},{1,5},{5,9},{9,13},{13,1},{2,6},{6,10},{... | collective-permute-start | bytes 786440 | tf_op jit(solution)/shard_map/ppermute | solution.py:18
  56.4 0.8 copy-start.1
  57.2 0.8 copy-start.3
  59.0 8.1 %collective-permute-start.7 = (bf16[4,512,256]{2,1,0:T(8,128)(2,1)S(1)}, bf16[4,512,256]{2,1,0:T(8,128)(2,1)S(1)}, u32[]{:S(2)}, u32[]{:S(2)}) collective-permute-start(bf16[4,512,256]{2,1,0:T(8,128)(2,1)S(1)} %pad_maximum_fusion.own_ref), channel_id=1, source_target_pairs={{0,1},{1,0},{2,3},{3,2},{4,5},{5,4},{6,7},{7,6},{8,9},{9,8},{10,11... | collective-permute-start | bytes 3145736 | tf_op jit(solution)/shard_map/ppermute | solution.py:22
  62.0 5.0 %copy-start.11 = (bf16[2,96,512]{2,1,0:T(8,128)(2,1)}, bf16[2,96,512]{2,1,0:T(8,128)(2,1)S(1)}, u32[]{:S(2)}) copy-start(bf16[2,96,512]{2,1,0:T(8,128)(2,1)S(1)} %convert_add_fusion) | copy-start | bytes 589828
  62.0 11.9 %collective-permute-start.8 = (bf16[96,512]{1,0:T(8,128)(2,1)S(1)}, bf16[96,512]{1,0:T(8,128)(2,1)S(1)}, u32[]{:S(2)}, u32[]{:S(2)}) collective-permute-start(bf16[96,512]{1,0:T(8,128)(2,1)S(1)} %fusion.3), channel_id=1, source_target_pairs={{0,128},{64,192},{128,0},{192,64},{256,384},{320,448},{384,256},{4... | collective-permute-start | bytes 294920 | tf_op jit(solution)/shard_map/ppermute | solution.py:22
  67.1 1.0 copy-start.2
  68.1 1.0 copy-start.4
  72.5 0.8 copy-start.5
  73.3 0.7 copy-start.6
  74.0 23.2 %copy-start.10 = (bf16[1,4096,128]{2,1,0:T(8,128)(2,1)S(1)}, bf16[1,4096,128]{2,1,0:T(8,128)(2,1)}, u32[]{:S(2)}) copy-start(bf16[1,4096,128]{2,1,0:T(8,128)(2,1)} %param.15) | copy-start | bytes 3145732
  74.0 13.0 %all-to-all-start.1 = ((bf16[4,128,512]{2,1,0:T(8,128)(2,1)}), bf16[4,128,512]{2,1,0:T(8,128)(2,1)S(1)}, u32[]{:S(2)}, u32[]{:S(2)}) async-start(bf16[4,128,512]{2,1,0:T(8,128)(2,1)} %copy-done.5), calls=%async_computation.1 | async-start | bytes 1048576 | tf_op jit(solution)/shard_map/all_to_all | solution.py:26
  79.8 17.5 %collective-permute-start.10 = (bf16[96,512]{1,0:T(8,128)(2,1)S(1)}, bf16[96,512]{1,0:T(8,128)(2,1)S(1)}, u32[]{:S(2)}, u32[]{:S(2)}) collective-permute-start(bf16[96,512]{1,0:T(8,128)(2,1)S(1)} %fusion.1), channel_id=1, source_target_pairs={{0,256},{64,320},{128,384},{192,448},{256,0},{320,64},{384,128},{4... | collective-permute-start | bytes 294920 | tf_op jit(solution)/shard_map/ppermute | solution.py:22
  88.1 15.1 %collective-permute-start.9 = (bf16[64,512]{1,0:T(8,128)(2,1)S(1)}, bf16[64,512]{1,0:T(8,128)(2,1)S(1)}, u32[]{:S(2)}, u32[]{:S(2)}) collective-permute-start(bf16[64,512]{1,0:T(8,128)(2,1)S(1)} %fusion.2), channel_id=1, source_target_pairs={{0,2},{2,0},{1,3},{3,1},{4,6},{6,4},{5,7},{7,5},{8,10},{10,8},{9,1... | collective-permute-start | bytes 196616 | tf_op jit(solution)/shard_map/ppermute | solution.py:22
  104.0 20.5 %all-to-all-start.2 = ((bf16[4,128,512]{2,1,0:T(8,128)(2,1)}), bf16[4,128,512]{2,1,0:T(8,128)(2,1)S(1)}, u32[]{:S(2)}, u32[]{:S(2)}) async-start(bf16[4,128,512]{2,1,0:T(8,128)(2,1)} %broadcast_in_dim.21), calls=%async_computation.2 | async-start | bytes 1048576 | tf_op jit(solution)/shard_map/all_to_all | solution.py:26
  107.5 37.8 %copy-start.15 = (f32[128,2]{0,1:T(2,128)S(1)}, f32[128,2]{0,1:T(2,128)}, u32[]{:S(2)}) copy-start(f32[128,2]{0,1:T(2,128)} %param.13) | copy-start | bytes 3076
  107.5 17.0 %collective-permute-start.11 = (bf16[1024,128]{1,0:T(8,128)(2,1)S(1)}, bf16[1024,128]{1,0:T(8,128)(2,1)S(1)}, u32[]{:S(2)}, u32[]{:S(2)}) collective-permute-start(bf16[1024,128]{1,0:T(8,128)(2,1)S(1)} %get-tuple-element.76), channel_id=1, source_target_pairs={{0,32},{16,48},{32,0},{48,16},{1,33},{17,49},{33,1},{49,17},{2,34}... | collective-permute-start | bytes 786440 | tf_op jit(solution)/shard_map/ppermute | solution.py:18
  111.2 13.3 %collective-permute-start.12 = (bf16[1024,128]{1,0:T(8,128)(2,1)S(1)}, bf16[1024,128]{1,0:T(8,128)(2,1)S(1)}, u32[]{:S(2)}, u32[]{:S(2)}) collective-permute-start(bf16[1024,128]{1,0:T(8,128)(2,1)S(1)} %get-tuple-element.77), channel_id=1, source_target_pairs={{0,16},{16,32},{32,48},{48,0},{1,17},{17,33},{33,49},{49,1},{2,18}... | collective-permute-start | bytes 786440 | tf_op jit(solution)/shard_map/ppermute | solution.py:18
  114.7 9.8 %collective-permute-start.13 = (bf16[1024,128]{1,0:T(8,128)(2,1)S(1)}, bf16[1024,128]{1,0:T(8,128)(2,1)S(1)}, u32[]{:S(2)}, u32[]{:S(2)}) collective-permute-start(bf16[1024,128]{1,0:T(8,128)(2,1)S(1)} %get-tuple-element.78), channel_id=1, source_target_pairs={{0,48},{16,0},{32,16},{48,32},{1,49},{17,1},{33,17},{49,33},{2,50}... | collective-permute-start | bytes 786440 | tf_op jit(solution)/shard_map/ppermute | solution.py:18
  117.1 7.4 %collective-permute-start.14 = (bf16[96,512]{1,0:T(8,128)(2,1)S(1)}, bf16[96,512]{1,0:T(8,128)(2,1)S(1)}, u32[]{:S(2)}, u32[]{:S(2)}) collective-permute-start(bf16[96,512]{1,0:T(8,128)(2,1)S(1)} %multiply_convert_fusion), channel_id=1, source_target_pairs={{0,128},{64,192},{128,0},{192,64},{256,384},{320,448},{384,256},{4... | collective-permute-start | bytes 294920 | tf_op jit(solution)/shard_map/ppermute | solution.py:22
  124.6 8.6 %collective-permute-start.15 = (bf16[4,128,512]{2,1,0:T(8,128)(2,1)S(1)}, bf16[4,128,512]{2,1,0:T(8,128)(2,1)S(1)}, u32[]{:S(2)}, u32[]{:S(2)}) collective-permute-start(bf16[4,128,512]{2,1,0:T(8,128)(2,1)S(1)} %all-to-all-done.2.own_ref), channel_id=1, source_target_pairs={{0,1},{1,0},{2,3},{3,2},{4,5},{5,4},{6,7},{7,6},{8,9},{9,8},{10,11... | collective-permute-start | bytes 1572872 | tf_op jit(solution)/shard_map/ppermute | solution.py:22
  126.5 12.1 %collective-permute-start.16 = (bf16[2,96,512]{2,1,0:T(8,128)(2,1)S(1)}, bf16[2,96,512]{2,1,0:T(8,128)(2,1)S(1)}, u32[]{:S(2)}, u32[]{:S(2)}) collective-permute-start(bf16[2,96,512]{2,1,0:T(8,128)(2,1)S(1)} %pad_maximum_fusion.4), channel_id=1, source_target_pairs={{0,64},{64,0},{128,192},{192,128},{256,320},{320,256},{384,448},{4... | collective-permute-start | bytes 589832 | tf_op jit(solution)/shard_map/ppermute | solution.py:22
  138.7 14.4 %all-to-all-start.3 = ((bf16[4,512,128]{2,1,0:T(8,128)(2,1)}), bf16[4,512,128]{2,1,0:T(8,128)(2,1)S(1)}, u32[]{:S(2)}, u32[]{:S(2)}) async-start(bf16[4,512,128]{2,1,0:T(8,128)(2,1)} %get-tuple-element.88), calls=%async_computation.3 | async-start | bytes 1048576 | tf_op jit(solution)/shard_map/all_to_all | solution.py:26
  153.8 16.9 %all-to-all-start.4 = ((bf16[8,64,128]{2,1,0:T(8,128)(2,1)}), bf16[8,64,128]{2,1,0:T(8,128)(2,1)S(1)}, u32[]{:S(2)}, u32[]{:S(2)}) async-start(bf16[8,64,128]{2,1,0:T(8,128)(2,1)} %bitcast.39), calls=%async_computation.4 | async-start | bytes 262144 | tf_op jit(solution)/shard_map/all_to_all | solution.py:26

commit v2 on v1

v2 whole, which is shorter than its diff:
```python
import jax
import jax.numpy as jnp
from jax import lax
from jax.experimental import pallas as pl
from jax.experimental.pallas import tpu as pltpu
from jax.sharding import Mesh
from jax.sharding import PartitionSpec as P

SIDE = 4
GATE_ORDER = (0, 1, 3, 2)
ROWS_ORDER = (0, 1, 2, 3)
VMEM = 24 * 1024 * 1024
BF16, F32 = jnp.bfloat16, jnp.float32
SHARD = ("x", "y", "zh", "c")


def shift(array, axis, step):
    size = lax.axis_size(axis)
    return lax.ppermute(array, axis, [(i, (i + step) % size) for i in range(size)])


def flip(array, axis, bit=1):
    return lax.ppermute(array, axis, [(i, i ^ bit) for i in range(lax.axis_size(axis))])


def exchange(blocks, axis):
    return lax.all_to_all(blocks, axis, split_axis=0, concat_axis=0, tiled=True)


def gather(block, axis):
    size = lax.axis_size(axis)
    return exchange(jnp.broadcast_to(block[None], (size,) + block.shape), axis)


def to_peers(cuts, order):
    return [shift(cuts[step], "x", step) if step else cuts[step] for step in order]


def in_hbm(array):
    return pltpu.with_memory_space_constraint(array, pltpu.HBM)


def call(kernel, out_shape, at, *arrays, spaces=None, out_spaces=None, scratch=()):
    spaces = spaces or [pltpu.VMEM] * len(arrays)
    out_spaces = out_spaces or [pltpu.VMEM] * len(out_shape)
    return pl.pallas_call(
        kernel,
        out_shape=out_shape,
        in_specs=[pl.BlockSpec(memory_space=space) for space in [pltpu.SMEM] + list(spaces)],
        out_specs=[pl.BlockSpec(memory_space=space) for space in out_spaces],
        scratch_shapes=list(scratch),
        compiler_params=pltpu.CompilerParams(vmem_limit_bytes=VMEM),
    )(at, *arrays)


def route_kernel(
    at_ref, routes_hbm, tokens_hbm, slotted_ref, pick_ref, routes_ref, tokens_ref, sems
):
    reads = [
        pltpu.make_async_copy(routes_hbm, routes_ref, sems.at[0]),
        pltpu.make_async_copy(tokens_hbm, tokens_ref, sems.at[1]),
    ]
    for read in reads:
        read.start()
    for read in reads:
        read.wait()
    rows = tokens_ref.shape[0]
    slots = slotted_ref.shape[0] // 2
    experts = 8
    capacity = slots // experts
    label = lax.broadcasted_iota(jnp.int32, (experts, rows), 0)
    first = (routes_ref[0:1, :] == label).astype(F32)
    second = (routes_ref[1:2, :] == label).astype(F32)
    named = first + second
    earlier = (
        lax.broadcasted_iota(jnp.int32, (rows, rows), 0)
        < lax.broadcasted_iota(jnp.int32, (rows, rows), 1)
    ).astype(F32)
    before = jnp.dot(named, earlier, preferred_element_type=F32).astype(jnp.int32)
    position = lax.broadcasted_iota(jnp.int32, (capacity, rows), 0)
    members = []
    for e in range(experts):
        hit = (before[e : e + 1] == position).astype(F32)
        span = slice(e * capacity, (e + 1) * capacity)
        pick_ref[span, :rows] = (hit * first[e : e + 1]).astype(BF16)
        pick_ref[span, rows:] = (hit * second[e : e + 1]).astype(BF16)
        members.append((hit * named[e : e + 1]).astype(BF16))
    slotted = jnp.dot(
        jnp.concatenate(members, axis=0), tokens_ref[...], preferred_element_type=F32
    ).astype(BF16)
    slotted_ref[:slots] = slotted
    slotted_ref[slots:] = slotted


def split_kernel(
    at_ref, gate_ref, key_hbm, first_hbm, second_hbm, down_hbm,
    c0, c1, c2, c3, keep_ref, give_ref, lower_ref, key_ref, first_ref, second_ref, sems,
):
    copies = [
        pltpu.make_async_copy(source, target, sems.at[i])
        for i, (source, target) in enumerate(
            (
                (key_hbm, key_ref),
                (first_hbm, first_ref),
                (second_hbm, second_ref),
                (down_hbm.at[:, 1 - at_ref[2]], lower_ref),
            )
        )
    ]
    for copy in copies:
        copy.start()
    wide, cols = gate_ref.shape[1] // SIDE, gate_ref.shape[0]
    for step, out_ref in enumerate((c0, c1, c2, c3)):
        x = lax.rem(at_ref[0] + step, SIDE)
        for j in range(wide // 128):
            lanes = pl.ds(pl.multiple_of(x * wide + j * 128, 128), 128)
            out_ref[j * cols : (j + 1) * cols, :] = gate_ref[:, lanes]
    for copy in copies[:3]:
        copy.wait()
    middle = first_ref.shape[0] // 2
    top = jnp.concatenate([key_ref[...], first_ref[:middle].astype(BF16)], axis=0)
    bottom = jnp.concatenate(
        [first_ref[middle:].astype(BF16), second_ref[...].astype(BF16)], axis=0
    )
    even = jnp.full(top.shape, at_ref[3], jnp.int32) == 0
    keep_ref[...] = jnp.where(even, top, bottom)
    give_ref[...] = jnp.where(even, bottom, top)
    copies[3].wait()


def gate_kernel(
    at_ref, w0, w1, w2, w3, own_ref, other_ref, here_ref, out_hbm, out_ref, sems
):
    rows = jnp.concatenate(
        [ref[y, half] for ref in (own_ref, other_ref) for y in range(SIDE) for half in range(2)],
        axis=1,
    )
    writes = []
    for k, (step, w_ref) in enumerate(zip(GATE_ORDER, (w0, w1, w2, w3))):
        x = lax.rem(at_ref[0] + SIDE - step, SIDE)
        parts = []
        for core in (at_ref[2], 1 - at_ref[2]):
            for y in ROWS_ORDER:
                for half in range(2):
                    j = lax.rem(at_ref[1] + y, SIDE) * 4 + half * 2 + core
                    parts.append(w_ref[pl.ds(pl.multiple_of(j * 128, 128), 128), :])
        total = lax.dot_general(
            jnp.concatenate(parts, axis=1),
            rows,
            (((1,), (1,)), ((), ())),
            preferred_element_type=F32,
        )
        out_ref[k] = total.astype(BF16)
        writes.append(pltpu.make_async_copy(out_ref.at[k], out_hbm.at[x], sems.at[k]))
        writes[-1].start()
        if step == 0:
            here_ref[...] = total
    for write in writes:
        write.wait()


def down_kernel(
    at_ref, down_hbm, other_ref, hidden_ref, mine_ref, theirs_ref, own_ref, sem
):
    read = pltpu.make_async_copy(down_hbm.at[:, at_ref[2]], own_ref, sem)
    read.start()
    chips, rows, wide = hidden_ref.shape
    hidden = jnp.concatenate([hidden_ref[i] for i in range(chips)], axis=1)
    read.wait()
    lower = jnp.concatenate(
        [ref[...].reshape(chips * wide, wide) for ref in (own_ref, other_ref)], axis=1
    )
    total = jnp.dot(hidden, lower, preferred_element_type=F32)
    mine_ref[...] = total[:, :wide]
    theirs_ref[...] = total[:, wide:]


def add_back(here, got, x):
    for step in range(SIDE):
        here = here + jnp.where(x == step, 0.0, got[step].astype(F32))
    return here


def body(
    key_weights, first_moment, second_moment, tokens, routes, route_weights, gate_up, down_proj
):
    branches = lax.axis_size("b")
    half, x, core = lax.axis_index("zh"), lax.axis_index("x"), lax.axis_index("c")
    branch = lax.axis_index("b")
    low, mid = branch % 2, (branch // 2) % 2
    at = jnp.stack([x, lax.axis_index("y"), core, low]).astype(jnp.int32)
    group_rows, width = tokens.shape
    capacity = 4 * group_rows // branches
    slots = branches * capacity
    hidden_here = gate_up.shape[2]
    rows_here = key_weights.shape[1]

    slotted, pick = call(
        route_kernel,
        [
            jax.ShapeDtypeStruct((2 * slots, width), BF16),
            jax.ShapeDtypeStruct((slots, 2 * group_rows), BF16),
        ],
        at,
        in_hbm(routes.T),
        in_hbm(tokens),
        spaces=[pltpu.HBM] * 2,
        scratch=[
            pltpu.VMEM(routes.T.shape, jnp.int32),
            pltpu.VMEM(tokens.shape, BF16),
            pltpu.SemaphoreType.DMA((2,)),
        ],
    )
    arrived = exchange(slotted.reshape(2 * branches, capacity, width), ("zh", "b"))

    gate_w = gate_up[0].reshape(2 * hidden_here, -1)
    columns = key_weights.shape[2]
    cut = jax.ShapeDtypeStruct((gate_w.size // SIDE // width, width), BF16)
    part = jax.ShapeDtypeStruct((3 * rows_here // 2, columns), BF16)
    lower = down_proj[0].reshape(-1, 2, hidden_here, width)
    *cuts, keep, give, other_lower = call(
        split_kernel,
        [cut] * SIDE + [part] * 2 + [jax.ShapeDtypeStruct((lower.shape[0],) + lower.shape[2:], BF16)],
        at,
        gate_w,
        in_hbm(key_weights[0]),
        in_hbm(first_moment[0]),
        in_hbm(second_moment[0]),
        in_hbm(lower),
        spaces=[pltpu.VMEM] + [pltpu.HBM] * 4,
        scratch=[
            pltpu.VMEM((rows_here, columns), BF16),
            pltpu.VMEM((rows_here, columns), F32),
            pltpu.VMEM((rows_here, columns), F32),
            pltpu.SemaphoreType.DMA((4,)),
        ],
    )
    weights = to_peers(cuts, GATE_ORDER)
    other_lower = flip(other_lower, "c")

    rows = arrived.reshape(2, slots, width)
    line = [rows] + [shift(rows, "y", -ahead) for ahead in ROWS_ORDER[1:]]
    line, weights, give = lax.optimization_barrier((line, weights, give))
    line = jnp.stack(line)
    line_other = flip(line, "c")
    got = flip(give, "b", 1)

    cols = 2 * hidden_here
    here, others = call(
        gate_kernel,
        [jax.ShapeDtypeStruct((cols, slots), F32), pltpu.HBM((SIDE, cols, slots), BF16)],
        at,
        *weights,
        line,
        line_other,
        out_spaces=[pltpu.VMEM, pltpu.HBM],
        scratch=[pltpu.VMEM((SIDE, cols, slots), BF16), pltpu.SemaphoreType.DMA((SIDE,))],
    )
    others, keep, got = lax.optimization_barrier((others, keep, got))
    slabs = (keep.astype(F32) + got.astype(F32)).reshape(2, -1, columns)
    give = lax.dynamic_index_in_dim(slabs, 1 - mid, 0, keepdims=False).astype(BF16)
    keep = lax.dynamic_index_in_dim(slabs, mid, 0, keepdims=False).astype(BF16)
    got = flip(give, "b", 2)
    gated = add_back(here, exchange(others, "x"), x)
    hidden = (jax.nn.silu(gated[:hidden_here]) * gated[hidden_here:]).astype(BF16)

    swap = flip(hidden, "zh")
    swap, got = lax.optimization_barrier((swap, got))

    both = jnp.where(
        half == 0,
        jnp.concatenate([hidden, swap], axis=0),
        jnp.concatenate([swap, hidden], axis=0),
    )
    spread = gather(both.T, ("x", "y"))
    slabs = (keep.astype(F32) + got.astype(F32)).astype(BF16)
    got = flip(slabs, "b", 4)
    slabs = ((slabs.astype(F32) + got.astype(F32)) / branches).astype(BF16)
    got = flip(slabs, "b", 2)
    spread, slabs, got = lax.optimization_barrier((spread, slabs, got))

    mine, theirs = call(
        down_kernel,
        [jax.ShapeDtypeStruct((slots, width), F32)] * 2,
        at,
        in_hbm(lower),
        other_lower,
        spread,
        spaces=[pltpu.HBM] + [pltpu.VMEM] * 2,
        scratch=[pltpu.VMEM(other_lower.shape, BF16), pltpu.SemaphoreType.DMA],
    )
    out = (mine + flip(theirs, "c")).astype(BF16)
    out, slabs, got = lax.optimization_barrier((out, slabs, got))
    slabs = jnp.stack([jnp.where(mid == 0, slabs, got), jnp.where(mid == 0, got, slabs)])
    got = flip(slabs, "b", 1)
    back = exchange(out.reshape(branches, capacity, width), "b").reshape(slots, width)
    back, got = lax.optimization_barrier((back, got))
    slabs = jnp.stack([jnp.where(low == 0, slabs, got), jnp.where(low == 0, got, slabs)])
    slabs = slabs.reshape(3 * rows_here, -1)
    picked = lax.dot_general(
        pick, back, (((0,), (0,)), ((), ())), preferred_element_type=F32
    )
    mixed = (
        route_weights[:, 0:1] * picked[:group_rows] + route_weights[:, 1:2] * picked[group_rows:]
    ).astype(BF16)
    return (
        slabs[:rows_here],
        slabs[rows_here : 2 * rows_here].astype(F32),
        slabs[2 * rows_here :].astype(F32),
        mixed,
    )


def solution(mesh):
    fine = Mesh(mesh.devices.reshape(8, SIDE, SIDE, 2, 2), ("b",) + SHARD)
    return jax.shard_map(
        body,
        mesh=fine,
        in_specs=(
            P("b", SHARD, None),
            P("b", SHARD, None),
            P("b", SHARD, None),
            P("b", SHARD),
            P("b", None),
            P("b", None),
            P("b", None, SHARD, None),
            P("b", None, SHARD),
        ),
        out_specs=(P(SHARD, None), P(SHARD, None), P(SHARD, None), P("b", SHARD)),
        check_vma=False,
    )
```

time: 175 us -> 162 us (0.926); the launches traced: 172 us -> 161 us
  starting transfers between devices: 103 us -> 85.7 us
  waiting for transfers between devices: 41.1 us -> 52.5 us
  local copies, waits for them, and re-layouts: 10.9 us -> 4.15 us
  Pallas kernels: 9.39 us -> 11.7 us
    ppermute x8 -> x9, waiting for transfers between devices: 13.8 us -> 36.1 us  [flip(): lax.ppermute(array, axis, [(i, i ^ bit) for i in range(lax.axis_size(axis...]
    all_to_all x5 -> x4, waiting for transfers between devices: 18.9 us -> 9.02 us  [exchange(): return lax.all_to_all(blocks, axis, split_axis=0, concat_axis=0, tiled=True)]
    ppermute x9 -> x6, starting transfers between devices: 29 us -> 19.5 us  [shift(): lax.ppermute(array, axis, [(i, (i + step) % size) for i in range(size)])]
    unnamed x32 -> x6, local copies, waits for them, and re-layouts: 8.92 us -> 2.24 us
    all_to_all x5 -> x4, starting transfers between devices: 35.7 us -> 30.5 us  [exchange(): return lax.all_to_all(blocks, axis, split_axis=0, concat_axis=0, tiled=True)]
    ppermute x8 -> x9, starting transfers between devices: 38.3 us -> 35.7 us  [flip(): lax.ppermute(array, axis, [(i, i ^ bit) for i in range(lax.axis_size(axis...]
    pallas_call x4, Pallas kernels: 9.39 us -> 11.7 us  [call(): pl.pallas_call(kernel, out_shape=out_shape, in_specs=[pl.BlockSpec(memory...]
    ppermute x9 -> x6, waiting for transfers between devices: 8.43 us -> 7.34 us  [shift(): lax.ppermute(array, axis, [(i, (i + step) % size) for i in range(size)])]
  transfers between devices with their start and end apart: 22 -> 19, of which waited for: 9 -> 11; matrix products, arithmetic and copies ran while one was open for 3% -> 1% of each run, Pallas kernels for 5% -> 4%
where the time goes in v2:
time: 162 us; the launch traced here: 161 us
  starting transfers between devices  85.7 us (53%)
  waiting for transfers between devices  52.5 us (32%)
  Pallas kernels  11.7 us (7%)
  other arithmetic  5.62 us (3%)
  local copies, waits for them, and re-layouts  4.15 us (3%)
    ppermute x9, waiting for transfers between devices, flip(): lax.ppermute(array, axis, [(i, i ^ bit) for i in range(lax.axis_size(axis...  36.1 us
    ppermute x9, starting transfers between devices, flip(): lax.ppermute(array, axis, [(i, i ^ bit) for i in range(lax.axis_size(axis...  35.7 us
    all_to_all x4, starting transfers between devices, exchange(): return lax.all_to_all(blocks, axis, split_axis=0, concat_axis=0, tiled=True)  30.5 us
    ppermute x6, starting transfers between devices, shift(): lax.ppermute(array, axis, [(i, (i + step) % size) for i in range(size)])  19.5 us
    pallas_call x4, Pallas kernels, call(): pl.pallas_call(kernel, out_shape=out_shape, in_specs=[pl.BlockSpec(memory...  11.7 us
    all_to_all x4, waiting for transfers between devices, exchange(): return lax.all_to_all(blocks, axis, split_axis=0, concat_axis=0, tiled=True)  9.02 us
    ppermute x6, waiting for transfers between devices, shift(): lax.ppermute(array, axis, [(i, (i + step) % size) for i in range(size)])  7.34 us
  transfers between devices with their start and end apart: 19, of which 11 were waited for; matrix products, arithmetic and copies ran while one was open for 1% of the time, Pallas kernels for 4%

profile of v2, /device:TPU:6, one launch (start us, length us, event | category | flops | bytes accessed | tf_op | source)
XLA Modules:
  0.0 160.9 jit_solution(11548508484618398614)
XLA Ops:
  0.6 0.1 pad_add_fusion.at_ref
  0.7 2.4 %shard_map.112 = (bf16[1024,128]{1,0:T(8,128)(2,1)}, bf16[512,256]{1,0:T(8,128)(2,1)S(1)}) custom-call(s32[4]{0:T(128)S(1)} %pad_add_fusion.at_ref, s32[2,128]{1,0:T(2,128)} %bitcast.70, bf16[128,128]{1,0:T(8,128)(2,1)} %tokens_hbm.1), custom_call_target="tpu_custom_call" | custom-call | tf_op jit(solution)/shard_map/pallas_call | solution.py:46
  3.1 15.3 %all-to-all-start = ((bf16[16,64,128]{2,1,0:T(8,128)(2,1)}), bf16[16,64,128]{2,1,0:T(8,128)(2,1)}, u32[]{:S(2)}, u32[]{:S(2)}) async-start(bf16[16,64,128]{2,1,0:T(8,128)(2,1)} %bitcast.10), calls=%async_computation | async-start | bytes 524288 | tf_op jit(solution)/shard_map/all_to_all | solution.py:27
  18.4 0.0 copy-start
  18.4 1.6 copy-done
  20.0 3.0 %shard_map.111 = (bf16[2048,128]{1,0:T(8,128)(2,1)S(1)}, bf16[2048,128]{1,0:T(8,128)(2,1)}, bf16[2048,128]{1,0:T(8,128)(2,1)}, bf16[2048,128]{1,0:T(8,128)(2,1)}...) custom-call(s32[4]{0:T(128)S(1)} %pad_add_fusion.at_ref, ...), custom_call_target="tpu_custom_call" | custom-call | tf_op jit(solution)/shard_map/pallas_call | solution.py:46
  23.0 2.4 %collective-permute-start.4 = (bf16[2048,128]{1,0:T(8,128)(2,1)}, bf16[2048,128]{1,0:T(8,128)(2,1)S(1)}, u32[]{:S(2)}, u32[]{:S(2)}) collective-permute-start(bf16[2048,128]{1,0:T(8,128)(2,1)} %get-tuple-element.42), channel_id=1, source_target_pairs={{0,16},{16,32},{32,48},{48,0},{1,17},{17,33},{33,49},{49,1},{2,18}... | collective-permute-start | bytes 1572872 | tf_op jit(solution)/shard_map/ppermute | solution.py:19
  25.4 3.5 %collective-permute-start.5 = (bf16[2048,128]{1,0:T(8,128)(2,1)}, bf16[2048,128]{1,0:T(8,128)(2,1)S(1)}, u32[]{:S(2)}, u32[]{:S(2)}) collective-permute-start(bf16[2048,128]{1,0:T(8,128)(2,1)} %get-tuple-element.43), channel_id=1, source_target_pairs={{0,48},{16,0},{32,16},{48,32},{1,49},{17,1},{33,17},{49,33},{2,50}... | collective-permute-start | bytes 1572872 | tf_op jit(solution)/shard_map/ppermute | solution.py:19
  28.9 3.3 %collective-permute-start.6 = (bf16[2048,128]{1,0:T(8,128)(2,1)}, bf16[2048,128]{1,0:T(8,128)(2,1)S(1)}, u32[]{:S(2)}, u32[]{:S(2)}) collective-permute-start(bf16[2048,128]{1,0:T(8,128)(2,1)} %get-tuple-element.44), channel_id=1, source_target_pairs={{0,32},{16,48},{32,0},{48,16},{1,33},{17,49},{33,1},{49,17},{2,34}... | collective-permute-start | bytes 1572872 | tf_op jit(solution)/shard_map/ppermute | solution.py:19
  32.2 4.6 %all-to-all-done = bf16[16,64,128]{2,1,0:T(8,128)(2,1)} async-done(((bf16[16,64,128]{2,1,0:T(8,128)(2,1)}), bf16[16,64,128]{2,1,0:T(8,128)(2,1)}, u32[]{:S(2)}, u32[]{:S(2)}) %all-to-all-start) | async-done | bytes 262176 | tf_op jit(solution)/shard_map/all_to_all | solution.py:27
  36.8 4.9 %collective-permute-start.1 = (bf16[2,512,128]{2,1,0:T(8,128)(2,1)}, bf16[2,512,128]{2,1,0:T(8,128)(2,1)S(1)}, u32[]{:S(2)}, u32[]{:S(2)}) collective-permute-start(bf16[2,512,128]{2,1,0:T(8,128)(2,1)} %bitcast.11), channel_id=1, source_target_pairs={{0,12},{4,0},{8,4},{12,8},{1,13},{5,1},{9,5},{13,9},{2,14},{6,2},{... | collective-permute-start | bytes 786440 | tf_op jit(solution)/shard_map/ppermute | solution.py:19
  41.7 2.5 %collective-permute-start.2 = (bf16[2,512,128]{2,1,0:T(8,128)(2,1)}, bf16[2,512,128]{2,1,0:T(8,128)(2,1)S(1)}, u32[]{:S(2)}, u32[]{:S(2)}) collective-permute-start(bf16[2,512,128]{2,1,0:T(8,128)(2,1)} %bitcast.11), channel_id=1, source_target_pairs={{0,8},{4,12},{8,0},{12,4},{1,9},{5,13},{9,1},{13,5},{2,10},{6,14},... | collective-permute-start | bytes 786440 | tf_op jit(solution)/shard_map/ppermute | solution.py:19
  44.2 0.0 collective-permute-done.4.w1
  44.3 2.9 %collective-permute-start.3 = (bf16[2,512,128]{2,1,0:T(8,128)(2,1)}, bf16[2,512,128]{2,1,0:T(8,128)(2,1)S(1)}, u32[]{:S(2)}, u32[]{:S(2)}) collective-permute-start(bf16[2,512,128]{2,1,0:T(8,128)(2,1)} %bitcast.11), channel_id=1, source_target_pairs={{0,4},{4,8},{8,12},{12,0},{1,5},{5,9},{9,13},{13,1},{2,6},{6,10},{... | collective-permute-start | bytes 786440 | tf_op jit(solution)/shard_map/ppermute | solution.py:19
  47.1 5.9 %collective-permute-done.5.w2 = bf16[2048,128]{1,0:T(8,128)(2,1)S(1)} collective-permute-done((bf16[2048,128]{1,0:T(8,128)(2,1)}, bf16[2048,128]{1,0:T(8,128)(2,1)S(1)}, u32[]{:S(2)}, u32[]{:S(2)}) %collective-permute-start.5) | collective-permute-done | bytes 524320 | tf_op jit(solution)/shard_map/ppermute | solution.py:19
  53.1 0.0 collective-permute-done.6.w3
  53.1 0.0 collective-permute-done.1
  53.1 0.0 collective-permute-done.2
  53.1 1.4 collective-permute-done.3
  54.5 1.1 pad_maximum_fusion.own_ref
  55.6 1.9 %collective-permute-start.7 = (bf16[4,2,512,128]{3,2,1,0:T(8,128)(2,1)S(1)}, bf16[4,2,512,128]{3,2,1,0:T(8,128)(2,1)S(1)}, u32[]{:S(2)}, u32[]{:S(2)}) collective-permute-start(bf16[4,2,512,128]{3,2,1,0:T(8,128)(2,1)S(1)} %pad_maximum_fusion.own_ref), channel_id=1, source_target_pairs={{0,1},{1,0},{2,3},{3,2},{4,5},{5,4},{6,7},{7,6},{8,9},{9,8},{10,11... | collective-permute-start | bytes 3145736 | tf_op jit(solution)/shard_map/ppermute | solution.py:23
  57.5 6.7 %collective-permute-start.8 = (bf16[192,512]{1,0:T(8,128)(2,1)}, bf16[192,512]{1,0:T(8,128)(2,1)S(1)}, u32[]{:S(2)}, u32[]{:S(2)}) collective-permute-start(bf16[192,512]{1,0:T(8,128)(2,1)} %get-tuple-element.57), channel_id=1, source_target_pairs={{0,64},{64,0},{128,192},{192,128},{256,320},{320,256},{384,448},{4... | collective-permute-start | bytes 589832 | tf_op jit(solution)/shard_map/ppermute | solution.py:23
  64.2 0.0 collective-permute-done.7.other_ref
  64.3 4.0 %shard_map.113 = (f32[128,512]{1,0:T(8,128)S(1)}, bf16[4,128,512]{2,1,0:T(8,128)(2,1)}) custom-call(s32[4]{0:T(128)S(1)} %pad_add_fusion.at_ref, bf16[2048,128]{1,0:T(8,128)(2,1)S(1)} %get-tuple-element.46.w0, bf16[2048,128]{1,0:T(8,128)(2,1)S(1)} %collective-permute-done.4.w1, bf16[2048,128]{1,0:T(8,128)(2,1)S(1)} %collective-permute-done.5.w2, ...), custom_call_target="tpu_custom_call" | custom-call | tf_op jit(solution)/shard_map/pallas_call | solution.py:46
  68.3 1.7 %collective-permute-done.8 = bf16[192,512]{1,0:T(8,128)(2,1)S(1)} collective-permute-done((bf16[192,512]{1,0:T(8,128)(2,1)}, bf16[192,512]{1,0:T(8,128)(2,1)S(1)}, u32[]{:S(2)}, u32[]{:S(2)}) %collective-permute-start.8) | collective-permute-done | bytes 196640 | tf_op jit(solution)/shard_map/ppermute | solution.py:23
  70.0 4.8 %all-to-all-start.1 = ((bf16[4,128,512]{2,1,0:T(8,128)(2,1)}), bf16[4,128,512]{2,1,0:T(8,128)(2,1)S(1)}, u32[]{:S(2)}, u32[]{:S(2)}) async-start(bf16[4,128,512]{2,1,0:T(8,128)(2,1)} %get-tuple-element.58), calls=%async_computation.1 | async-start | bytes 1048576 | tf_op jit(solution)/shard_map/all_to_all | solution.py:27
  74.8 0.1 convert_add_fusion
  74.8 0.0 copy-start.1
  74.9 0.6 copy-done.1
  75.5 3.8 %collective-permute-start.10 = (bf16[96,512]{1,0:T(8,128)(2,1)S(1)}, bf16[96,512]{1,0:T(8,128)(2,1)S(1)}, u32[]{:S(2)}, u32[]{:S(2)}) collective-permute-start(bf16[96,512]{1,0:T(8,128)(2,1)S(1)} %fusion.3), channel_id=1, source_target_pairs={{0,128},{64,192},{128,0},{192,64},{256,384},{320,448},{384,256},{4... | collective-permute-start | bytes 294920 | tf_op jit(solution)/shard_map/ppermute | solution.py:23
  79.4 2.9 %all-to-all-done.1 = bf16[4,128,512]{2,1,0:T(8,128)(2,1)S(1)} async-done(((bf16[4,128,512]{2,1,0:T(8,128)(2,1)}), bf16[4,128,512]{2,1,0:T(8,128)(2,1)S(1)}, u32[]{:S(2)}, u32[]{:S(2)}) %all-to-all-start.1) | async-done | bytes 524320 | tf_op jit(solution)/shard_map/all_to_all | solution.py:27
  82.3 0.1 bitcast_add_fusion
  82.4 8.5 %collective-permute-start.9 = (bf16[64,512]{1,0:T(8,128)(2,1)S(1)}, bf16[64,512]{1,0:T(8,128)(2,1)S(1)}, u32[]{:S(2)}, u32[]{:S(2)}) collective-permute-start(bf16[64,512]{1,0:T(8,128)(2,1)S(1)} %fusion.1), channel_id=1, source_target_pairs={{0,2},{2,0},{1,3},{3,1},{4,6},{6,4},{5,7},{7,5},{8,10},{10,8},{9,1... | collective-permute-start | bytes 196616 | tf_op jit(solution)/shard_map/ppermute | solution.py:23
  90.9 0.0 collective-permute-done.10
  90.9 9.2 %collective-permute-done.9 = bf16[64,512]{1,0:T(8,128)(2,1)S(1)} collective-permute-done((bf16[64,512]{1,0:T(8,128)(2,1)S(1)}, bf16[64,512]{1,0:T(8,128)(2,1)S(1)}, u32[]{:S(2)}, u32[]{:S(2)}) %collective-permute-start.9) | collective-permute-done | bytes 65568 | tf_op jit(solution)/shard_map/ppermute | solution.py:23
  100.2 0.1 copy.12
  100.3 1.8 %broadcast_in_dim.14 = bf16[16,512,128]{2,1,0:T(8,128)(2,1)} broadcast(bf16[512,128]{1,0:T(8,128)(2,1)S(1)} %copy.12), dimensions={1,2} | broadcast | bytes 2228224 | tf_op jit(solution)/shard_map/broadcast_in_dim | solution.py:32
  102.1 5.6 %all-to-all-start.2 = ((bf16[16,512,128]{2,1,0:T(8,128)(2,1)}), bf16[16,512,128]{2,1,0:T(8,128)(2,1)S(1)}, u32[]{:S(2)}, u32[]{:S(2)}) async-start(bf16[16,512,128]{2,1,0:T(8,128)(2,1)} %broadcast_in_dim.14), calls=%async_computation.2 | async-start | bytes 4194304 | tf_op jit(solution)/shard_map/all_to_all | solution.py:27
  107.7 1.9 %collective-permute-start = (bf16[32,64,128]{2,1,0:T(8,128)(2,1)S(1)}, bf16[32,64,128]{2,1,0:T(8,128)(2,1)S(1)}, u32[]{:S(2)}, u32[]{:S(2)}) collective-permute-start(bf16[32,64,128]{2,1,0:T(8,128)(2,1)S(1)} %get-tuple-element.39), channel_id=1, source_target_pairs={{0,1},{1,0},{2,3},{3,2},{4,5},{5,4},{6,7},{7,6},{8,9},{9,8},{10,11... | collective-permute-start | bytes 1572872 | tf_op jit(solution)/shard_map/ppermute | solution.py:23
  109.7 0.9 fusion
  110.6 5.0 %collective-permute-start.11 = (bf16[96,512]{1,0:T(8,128)(2,1)S(1)}, bf16[96,512]{1,0:T(8,128)(2,1)S(1)}, u32[]{:S(2)}, u32[]{:S(2)}) collective-permute-start(bf16[96,512]{1,0:T(8,128)(2,1)S(1)} %fusion), channel_id=1, source_target_pairs={{0,256},{64,320},{128,384},{192,448},{256,0},{320,64},{384,128},{4... | collective-permute-start | bytes 294920 | tf_op jit(solution)/shard_map/ppermute | solution.py:23
  115.6 12.1 %collective-permute-done.11 = bf16[96,512]{1,0:T(8,128)(2,1)S(1)} collective-permute-done((bf16[96,512]{1,0:T(8,128)(2,1)S(1)}, bf16[96,512]{1,0:T(8,128)(2,1)S(1)}, u32[]{:S(2)}, u32[]{:S(2)}) %collective-permute-start.11) | collective-permute-done | bytes 98336 | tf_op jit(solution)/shard_map/ppermute | solution.py:23
  127.7 0.0 copy-start.2
  127.7 1.9 %collective-permute-start.12 = (bf16[96,512]{1,0:T(8,128)(2,1)S(1)}, bf16[96,512]{1,0:T(8,128)(2,1)}, u32[]{:S(2)}, u32[]{:S(2)}) collective-permute-start(bf16[96,512]{1,0:T(8,128)(2,1)S(1)} %multiply_convert_fusion), channel_id=1, source_target_pairs={{0,128},{64,192},{128,0},{192,64},{256,384},{320,448},{384,256},{4... | collective-permute-start | bytes 294920 | tf_op jit(solution)/shard_map/ppermute | solution.py:23
  129.7 5.8 %collective-permute-done.12 = bf16[96,512]{1,0:T(8,128)(2,1)} collective-permute-done((bf16[96,512]{1,0:T(8,128)(2,1)S(1)}, bf16[96,512]{1,0:T(8,128)(2,1)}, u32[]{:S(2)}, u32[]{:S(2)}) %collective-permute-start.12) | collective-permute-done | bytes 98336 | tf_op jit(solution)/shard_map/ppermute | solution.py:23
  135.4 0.0 all-to-all-done.2.hidden_ref
  135.5 0.0 collective-permute-done.other_ref
  135.5 2.3 %shard_map.114 = (f32[512,128]{1,0:T(8,128)S(1)}, f32[512,128]{1,0:T(8,128)S(1)}) custom-call(s32[4]{0:T(128)S(1)} %pad_add_fusion.at_ref, bf16[32,2,64,128]{3,2,1,0:T(8,128)(2,1)} %bitcast.59, bf16[32,64,128]{2,1,0:T(8,128)(2,1)S(1)} %collective-permute-done.other_ref, bf16[16,512,128]{2,1,0:T(8,128)(2,1)S(1)} %all-to-all-done.2.hidden_ref), custom_call_target="tpu_custom_call" | custom-call | tf_op jit(solution)/shard_map/pallas_call | solution.py:46
  137.8 1.9 %collective-permute-start.13 = (f32[512,128]{1,0:T(8,128)S(1)}, f32[512,128]{1,0:T(8,128)S(1)}, u32[]{:S(2)}, u32[]{:S(2)}) collective-permute-start(f32[512,128]{1,0:T(8,128)S(1)} %get-tuple-element.65), channel_id=1, source_target_pairs={{0,1},{1,0},{2,3},{3,2},{4,5},{5,4},{6,7},{7,6},{8,9},{9,8},{10,11... | collective-permute-start | bytes 786440 | tf_op jit(solution)/shard_map/ppermute | solution.py:23
  139.7 1.5 collective-permute-done.13
  141.2 0.7 add_convert_fusion
  141.9 4.8 %all-to-all-start.3 = ((bf16[8,64,128]{2,1,0:T(8,128)(2,1)}), bf16[8,64,128]{2,1,0:T(8,128)(2,1)S(1)}, u32[]{:S(2)}, u32[]{:S(2)}) async-start(bf16[8,64,128]{2,1,0:T(8,128)(2,1)} %bitcast.26), calls=%async_computation.3 | async-start | bytes 262144 | tf_op jit(solution)/shard_map/all_to_all | solution.py:27
  146.7 0.9 select_bitcast_fusion.3
  147.7 3.9 %collective-permute-start.14 = (bf16[2,96,512]{2,1,0:T(8,128)(2,1)S(1)}, bf16[2,96,512]{2,1,0:T(8,128)(2,1)S(1)}, u32[]{:S(2)}, u32[]{:S(2)}) collective-permute-start(bf16[2,96,512]{2,1,0:T(8,128)(2,1)S(1)} %pad_maximum_fusion.2), channel_id=1, source_target_pairs={{0,64},{64,0},{128,192},{192,128},{256,320},{320,256},{384,448},{4... | collective-permute-start | bytes 589832 | tf_op jit(solution)/shard_map/ppermute | solution.py:23
  151.6 0.0 copy-done.2
  151.6 5.8 %collective-permute-done.14 = bf16[2,96,512]{2,1,0:T(8,128)(2,1)S(1)} collective-permute-done((bf16[2,96,512]{2,1,0:T(8,128)(2,1)S(1)}, bf16[2,96,512]{2,1,0:T(8,128)(2,1)S(1)}, u32[]{:S(2)}, u32[]{:S(2)}) %collective-permute-start.14) | collective-permute-done | bytes 196640 | tf_op jit(solution)/shard_map/ppermute | solution.py:23
  157.5 1.5 all-to-all-done.3
  159.1 0.9 slice_convert_fusion
  159.9 0.3 fusion.7
  160.2 0.7 fusion.6
  (8 shorter events, 0.2 us)
Async XLA Ops:
  3.1 33.7 %all-to-all-start = ((bf16[16,64,128]{2,1,0:T(8,128)(2,1)}), bf16[16,64,128]{2,1,0:T(8,128)(2,1)}, u32[]{:S(2)}, u32[]{:S(2)}) async-start(bf16[16,64,128]{2,1,0:T(8,128)(2,1)} %bitcast.10), calls=%async_computation | async-start | bytes 524288 | tf_op jit(solution)/shard_map/all_to_all | solution.py:27
  18.4 1.6 copy-start
  23.0 21.2 %collective-permute-start.4 = (bf16[2048,128]{1,0:T(8,128)(2,1)}, bf16[2048,128]{1,0:T(8,128)(2,1)S(1)}, u32[]{:S(2)}, u32[]{:S(2)}) collective-permute-start(bf16[2048,128]{1,0:T(8,128)(2,1)} %get-tuple-element.42), channel_id=1, source_target_pairs={{0,16},{16,32},{32,48},{48,0},{1,17},{17,33},{33,49},{49,1},{2,18}... | collective-permute-start | bytes 1572872 | tf_op jit(solution)/shard_map/ppermute | solution.py:19
  25.4 27.7 %collective-permute-start.5 = (bf16[2048,128]{1,0:T(8,128)(2,1)}, bf16[2048,128]{1,0:T(8,128)(2,1)S(1)}, u32[]{:S(2)}, u32[]{:S(2)}) collective-permute-start(bf16[2048,128]{1,0:T(8,128)(2,1)} %get-tuple-element.43), channel_id=1, source_target_pairs={{0,48},{16,0},{32,16},{48,32},{1,49},{17,1},{33,17},{49,33},{2,50}... | collective-permute-start | bytes 1572872 | tf_op jit(solution)/shard_map/ppermute | solution.py:19
  28.9 24.2 %collective-permute-start.6 = (bf16[2048,128]{1,0:T(8,128)(2,1)}, bf16[2048,128]{1,0:T(8,128)(2,1)S(1)}, u32[]{:S(2)}, u32[]{:S(2)}) collective-permute-start(bf16[2048,128]{1,0:T(8,128)(2,1)} %get-tuple-element.44), channel_id=1, source_target_pairs={{0,32},{16,48},{32,0},{48,16},{1,33},{17,49},{33,1},{49,17},{2,34}... | collective-permute-start | bytes 1572872 | tf_op jit(solution)/shard_map/ppermute | solution.py:19
  36.8 16.3 %collective-permute-start.1 = (bf16[2,512,128]{2,1,0:T(8,128)(2,1)}, bf16[2,512,128]{2,1,0:T(8,128)(2,1)S(1)}, u32[]{:S(2)}, u32[]{:S(2)}) collective-permute-start(bf16[2,512,128]{2,1,0:T(8,128)(2,1)} %bitcast.11), channel_id=1, source_target_pairs={{0,12},{4,0},{8,4},{12,8},{1,13},{5,1},{9,5},{13,9},{2,14},{6,2},{... | collective-permute-start | bytes 786440 | tf_op jit(solution)/shard_map/ppermute | solution.py:19
  41.7 11.4 %collective-permute-start.2 = (bf16[2,512,128]{2,1,0:T(8,128)(2,1)}, bf16[2,512,128]{2,1,0:T(8,128)(2,1)S(1)}, u32[]{:S(2)}, u32[]{:S(2)}) collective-permute-start(bf16[2,512,128]{2,1,0:T(8,128)(2,1)} %bitcast.11), channel_id=1, source_target_pairs={{0,8},{4,12},{8,0},{12,4},{1,9},{5,13},{9,1},{13,5},{2,10},{6,14},... | collective-permute-start | bytes 786440 | tf_op jit(solution)/shard_map/ppermute | solution.py:19
  44.3 10.2 %collective-permute-start.3 = (bf16[2,512,128]{2,1,0:T(8,128)(2,1)}, bf16[2,512,128]{2,1,0:T(8,128)(2,1)S(1)}, u32[]{:S(2)}, u32[]{:S(2)}) collective-permute-start(bf16[2,512,128]{2,1,0:T(8,128)(2,1)} %bitcast.11), channel_id=1, source_target_pairs={{0,4},{4,8},{8,12},{12,0},{1,5},{5,9},{9,13},{13,1},{2,6},{6,10},{... | collective-permute-start | bytes 786440 | tf_op jit(solution)/shard_map/ppermute | solution.py:19
  55.6 8.7 %collective-permute-start.7 = (bf16[4,2,512,128]{3,2,1,0:T(8,128)(2,1)S(1)}, bf16[4,2,512,128]{3,2,1,0:T(8,128)(2,1)S(1)}, u32[]{:S(2)}, u32[]{:S(2)}) collective-permute-start(bf16[4,2,512,128]{3,2,1,0:T(8,128)(2,1)S(1)} %pad_maximum_fusion.own_ref), channel_id=1, source_target_pairs={{0,1},{1,0},{2,3},{3,2},{4,5},{5,4},{6,7},{7,6},{8,9},{9,8},{10,11... | collective-permute-start | bytes 3145736 | tf_op jit(solution)/shard_map/ppermute | solution.py:23
  57.5 12.5 %collective-permute-start.8 = (bf16[192,512]{1,0:T(8,128)(2,1)}, bf16[192,512]{1,0:T(8,128)(2,1)S(1)}, u32[]{:S(2)}, u32[]{:S(2)}) collective-permute-start(bf16[192,512]{1,0:T(8,128)(2,1)} %get-tuple-element.57), channel_id=1, source_target_pairs={{0,64},{64,0},{128,192},{192,128},{256,320},{320,256},{384,448},{4... | collective-permute-start | bytes 589832 | tf_op jit(solution)/shard_map/ppermute | solution.py:23
  70.0 12.3 %all-to-all-start.1 = ((bf16[4,128,512]{2,1,0:T(8,128)(2,1)}), bf16[4,128,512]{2,1,0:T(8,128)(2,1)S(1)}, u32[]{:S(2)}, u32[]{:S(2)}) async-start(bf16[4,128,512]{2,1,0:T(8,128)(2,1)} %get-tuple-element.58), calls=%async_computation.1 | async-start | bytes 1048576 | tf_op jit(solution)/shard_map/all_to_all | solution.py:27
  74.8 0.7 copy-start.1
  75.5 15.4 %collective-permute-start.10 = (bf16[96,512]{1,0:T(8,128)(2,1)S(1)}, bf16[96,512]{1,0:T(8,128)(2,1)S(1)}, u32[]{:S(2)}, u32[]{:S(2)}) collective-permute-start(bf16[96,512]{1,0:T(8,128)(2,1)S(1)} %fusion.3), channel_id=1, source_target_pairs={{0,128},{64,192},{128,0},{192,64},{256,384},{320,448},{384,256},{4... | collective-permute-start | bytes 294920 | tf_op jit(solution)/shard_map/ppermute | solution.py:23
  82.4 17.7 %collective-permute-start.9 = (bf16[64,512]{1,0:T(8,128)(2,1)S(1)}, bf16[64,512]{1,0:T(8,128)(2,1)S(1)}, u32[]{:S(2)}, u32[]{:S(2)}) collective-permute-start(bf16[64,512]{1,0:T(8,128)(2,1)S(1)} %fusion.1), channel_id=1, source_target_pairs={{0,2},{2,0},{1,3},{3,1},{4,6},{6,4},{5,7},{7,5},{8,10},{10,8},{9,1... | collective-permute-start | bytes 196616 | tf_op jit(solution)/shard_map/ppermute | solution.py:23
  102.1 33.4 %all-to-all-start.2 = ((bf16[16,512,128]{2,1,0:T(8,128)(2,1)}), bf16[16,512,128]{2,1,0:T(8,128)(2,1)S(1)}, u32[]{:S(2)}, u32[]{:S(2)}) async-start(bf16[16,512,128]{2,1,0:T(8,128)(2,1)} %broadcast_in_dim.14), calls=%async_computation.2 | async-start | bytes 4194304 | tf_op jit(solution)/shard_map/all_to_all | solution.py:27
  107.7 27.7 %collective-permute-start = (bf16[32,64,128]{2,1,0:T(8,128)(2,1)S(1)}, bf16[32,64,128]{2,1,0:T(8,128)(2,1)S(1)}, u32[]{:S(2)}, u32[]{:S(2)}) collective-permute-start(bf16[32,64,128]{2,1,0:T(8,128)(2,1)S(1)} %get-tuple-element.39), channel_id=1, source_target_pairs={{0,1},{1,0},{2,3},{3,2},{4,5},{5,4},{6,7},{7,6},{8,9},{9,8},{10,11... | collective-permute-start | bytes 1572872 | tf_op jit(solution)/shard_map/ppermute | solution.py:23
  110.6 17.1 %collective-permute-start.11 = (bf16[96,512]{1,0:T(8,128)(2,1)S(1)}, bf16[96,512]{1,0:T(8,128)(2,1)S(1)}, u32[]{:S(2)}, u32[]{:S(2)}) collective-permute-start(bf16[96,512]{1,0:T(8,128)(2,1)S(1)} %fusion), channel_id=1, source_target_pairs={{0,256},{64,320},{128,384},{192,448},{256,0},{320,64},{384,128},{4... | collective-permute-start | bytes 294920 | tf_op jit(solution)/shard_map/ppermute | solution.py:23
  127.7 23.9 %copy-start.2 = (f32[128,2]{0,1:T(2,128)S(1)}, f32[128,2]{0,1:T(2,128)}, u32[]{:S(2)}) copy-start(f32[128,2]{0,1:T(2,128)} %param.13) | copy-start | bytes 3076
  127.7 7.7 %collective-permute-start.12 = (bf16[96,512]{1,0:T(8,128)(2,1)S(1)}, bf16[96,512]{1,0:T(8,128)(2,1)}, u32[]{:S(2)}, u32[]{:S(2)}) collective-permute-start(bf16[96,512]{1,0:T(8,128)(2,1)S(1)} %multiply_convert_fusion), channel_id=1, source_target_pairs={{0,128},{64,192},{128,0},{192,64},{256,384},{320,448},{384,256},{4... | collective-permute-start | bytes 294920 | tf_op jit(solution)/shard_map/ppermute | solution.py:23
  137.8 3.4 %collective-permute-start.13 = (f32[512,128]{1,0:T(8,128)S(1)}, f32[512,128]{1,0:T(8,128)S(1)}, u32[]{:S(2)}, u32[]{:S(2)}) collective-permute-start(f32[512,128]{1,0:T(8,128)S(1)} %get-tuple-element.65), channel_id=1, source_target_pairs={{0,1},{1,0},{2,3},{3,2},{4,5},{5,4},{6,7},{7,6},{8,9},{9,8},{10,11... | collective-permute-start | bytes 786440 | tf_op jit(solution)/shard_map/ppermute | solution.py:23
  141.9 17.1 %all-to-all-start.3 = ((bf16[8,64,128]{2,1,0:T(8,128)(2,1)}), bf16[8,64,128]{2,1,0:T(8,128)(2,1)S(1)}, u32[]{:S(2)}, u32[]{:S(2)}) async-start(bf16[8,64,128]{2,1,0:T(8,128)(2,1)} %bitcast.26), calls=%async_computation.3 | async-start | bytes 262144 | tf_op jit(solution)/shard_map/all_to_all | solution.py:27
  147.7 9.8 %collective-permute-start.14 = (bf16[2,96,512]{2,1,0:T(8,128)(2,1)S(1)}, bf16[2,96,512]{2,1,0:T(8,128)(2,1)S(1)}, u32[]{:S(2)}, u32[]{:S(2)}) collective-permute-start(bf16[2,96,512]{2,1,0:T(8,128)(2,1)S(1)} %pad_maximum_fusion.2), channel_id=1, source_target_pairs={{0,64},{64,0},{128,192},{192,128},{256,320},{320,256},{384,448},{4... | collective-permute-start | bytes 589832 | tf_op jit(solution)/shard_map/ppermute | solution.py:23

commit v3 on v2

--- a/solution.py
+++ b/solution.py
@@ -93,9 +93,17 @@
 
 
 def split_kernel(
-    at_ref, gate_ref, key_hbm, first_hbm, second_hbm, down_hbm,
-    c0, c1, c2, c3, keep_ref, give_ref, lower_ref, key_ref, first_ref, second_ref, sems,
-):
+    at_ref, gate_hbm, key_hbm, first_hbm, second_hbm, down_hbm,
+    c0, c1, c2, c3, keep_ref, give_ref, lower_ref,
+    gate_ref, key_ref, first_ref, second_ref, gate_sems, sems,
+):
+    wide, cols = gate_ref.shape[2], gate_ref.shape[1]
+    reads = []
+    for step in range(SIDE):
+        lanes = pl.ds(pl.multiple_of(lax.rem(at_ref[0] + step, SIDE) * wide, wide), wide)
+        reads.append(
+            pltpu.make_async_copy(gate_hbm.at[:, lanes], gate_ref.at[step], gate_sems.at[step])
+        )
     copies = [
         pltpu.make_async_copy(source, target, sems.at[i])
         for i, (source, target) in enumerate(
@@ -107,14 +115,13 @@
             )
         )
     ]
-    for copy in copies:
+    for copy in reads + copies:
         copy.start()
-    wide, cols = gate_ref.shape[1] // SIDE, gate_ref.shape[0]
     for step, out_ref in enumerate((c0, c1, c2, c3)):
-        x = lax.rem(at_ref[0] + step, SIDE)
+        reads[step].wait()
         for j in range(wide // 128):
-            lanes = pl.ds(pl.multiple_of(x * wide + j * 128, 128), 128)
-            out_ref[j * cols : (j + 1) * cols, :] = gate_ref[:, lanes]
+            lanes = slice(j * 128, (j + 1) * 128)
+            out_ref[j * cols : (j + 1) * cols, :] = gate_ref[step, :, lanes]
     for copy in copies[:3]:
         copy.wait()
     middle = first_ref.shape[0] // 2
@@ -222,28 +229,31 @@
         split_kernel,
         [cut] * SIDE + [part] * 2 + [jax.ShapeDtypeStruct((lower.shape[0],) + lower.shape[2:], BF16)],
         at,
-        gate_w,
+        in_hbm(gate_w),
         in_hbm(key_weights[0]),
         in_hbm(first_moment[0]),
         in_hbm(second_moment[0]),
         in_hbm(lower),
-        spaces=[pltpu.VMEM] + [pltpu.HBM] * 4,
+        spaces=[pltpu.HBM] * 5,
         scratch=[
+            pltpu.VMEM((SIDE, gate_w.shape[0], gate_w.shape[1] // SIDE), BF16),
             pltpu.VMEM((rows_here, columns), BF16),
             pltpu.VMEM((rows_here, columns), F32),
             pltpu.VMEM((rows_here, columns), F32),
+            pltpu.SemaphoreType.DMA((SIDE,)),
             pltpu.SemaphoreType.DMA((4,)),
         ],
     )
     weights = to_peers(cuts, GATE_ORDER)
+    got = flip(give, "b", 1)
     other_lower = flip(other_lower, "c")
 
+    arrived, other_lower = lax.optimization_barrier((arrived, other_lower))
     rows = arrived.reshape(2, slots, width)
     line = [rows] + [shift(rows, "y", -ahead) for ahead in ROWS_ORDER[1:]]
-    line, weights, give = lax.optimization_barrier((line, weights, give))
+    line, weights, got = lax.optimization_barrier((line, weights, got))
     line = jnp.stack(line)
     line_other = flip(line, "c")
-    got = flip(give, "b", 1)
 
     cols = 2 * hidden_here
     here, others = call(
@@ -265,7 +275,8 @@
     hidden = (jax.nn.silu(gated[:hidden_here]) * gated[hidden_here:]).astype(BF16)
 
     swap = flip(hidden, "zh")
-    swap, got = lax.optimization_barrier((swap, got))
+    slabs = (keep.astype(F32) + got.astype(F32)).astype(BF16)
+    swap, slabs = lax.optimization_barrier((swap, slabs))
 
     both = jnp.where(
         half == 0,
@@ -273,7 +284,6 @@
         jnp.concatenate([swap, hidden], axis=0),
     )
     spread = gather(both.T, ("x", "y"))
-    slabs = (keep.astype(F32) + got.astype(F32)).astype(BF16)
     got = flip(slabs, "b", 4)
     slabs = ((slabs.astype(F32) + got.astype(F32)) / branches).astype(BF16)
     got = flip(slabs, "b", 2)

time: 162 us -> 170 us (1.049); the launches traced: 161 us -> 167 us
  starting transfers between devices: 85.7 us -> 105 us
  waiting for transfers between devices: 52.5 us -> 41.7 us
  local copies, waits for them, and re-layouts: 4.15 us -> 1.9 us
  other arithmetic: 5.62 us -> 3.83 us
    ppermute x9, waiting for transfers between devices: 36.1 us -> 24.3 us  [flip(): lax.ppermute(array, axis, [(i, i ^ bit) for i in range(lax.axis_size(axis...]
    all_to_all x4, starting transfers between devices: 30.5 us -> 41 us  [exchange(): return lax.all_to_all(blocks, axis, split_axis=0, concat_axis=0, tiled=True)]
    ppermute x9, starting transfers between devices: 35.7 us -> 42.6 us  [flip(): lax.ppermute(array, axis, [(i, i ^ bit) for i in range(lax.axis_size(axis...]
    unnamed x6 -> x2, local copies, waits for them, and re-layouts: 2.24 us -> 0.01 us
    ppermute x6, starting transfers between devices: 19.5 us -> 21.5 us  [shift(): lax.ppermute(array, axis, [(i, (i + step) % size) for i in range(size)])]
    ppermute x6, waiting for transfers between devices: 7.34 us -> 9.29 us  [shift(): lax.ppermute(array, axis, [(i, (i + step) % size) for i in range(size)])]
  transfers between devices with their start and end apart: 19 -> 19, of which waited for: 11 -> 11; matrix products, arithmetic and copies ran while one was open for 1% -> 0% of each run, Pallas kernels for 4% -> 2%
where the time goes in v3:
time: 170 us; the launch traced here: 167 us
  starting transfers between devices  105 us (62%)
  waiting for transfers between devices  41.7 us (25%)
  Pallas kernels  13.1 us (8%)
  other arithmetic  3.83 us (2%)
  local copies, waits for them, and re-layouts  1.9 us (1%)
    ppermute x9, starting transfers between devices, flip(): lax.ppermute(array, axis, [(i, i ^ bit) for i in range(lax.axis_size(axis...  42.6 us
    all_to_all x4, starting transfers between devices, exchange(): return lax.all_to_all(blocks, axis, split_axis=0, concat_axis=0, tiled=True)  41 us
    ppermute x9, waiting for transfers between devices, flip(): lax.ppermute(array, axis, [(i, i ^ bit) for i in range(lax.axis_size(axis...  24.3 us
    ppermute x6, starting transfers between devices, shift(): lax.ppermute(array, axis, [(i, (i + step) % size) for i in range(size)])  21.5 us
    pallas_call x4, Pallas kernels, call(): pl.pallas_call(kernel, out_shape=out_shape, in_specs=[pl.BlockSpec(memory...  13.1 us
    ppermute x6, waiting for transfers between devices, shift(): lax.ppermute(array, axis, [(i, (i + step) % size) for i in range(size)])  9.29 us
    all_to_all x4, waiting for transfers between devices, exchange(): return lax.all_to_all(blocks, axis, split_axis=0, concat_axis=0, tiled=True)  8.13 us
  transfers between devices with their start and end apart: 19, of which 11 were waited for; matrix products, arithmetic and copies ran while one was open for 0% of the time, Pallas kernels for 2%

profile of v3, /device:TPU:6, one launch (start us, length us, event | category | flops | bytes accessed | tf_op | source)
XLA Modules:
  0.0 166.8 jit_solution(17061067766229674760)
XLA Ops:
  0.6 0.1 pad_add_fusion.at_ref
  0.7 2.4 %shard_map.111 = (bf16[1024,128]{1,0:T(8,128)(2,1)}, bf16[512,256]{1,0:T(8,128)(2,1)S(1)}) custom-call(s32[4]{0:T(128)S(1)} %pad_add_fusion.at_ref, s32[2,128]{1,0:T(2,128)} %bitcast.70, bf16[128,128]{1,0:T(8,128)(2,1)} %tokens_hbm.1), custom_call_target="tpu_custom_call" | custom-call | tf_op jit(solution)/shard_map/pallas_call | solution.py:46
  3.1 15.3 %all-to-all-start = ((bf16[16,64,128]{2,1,0:T(8,128)(2,1)}), bf16[16,64,128]{2,1,0:T(8,128)(2,1)}, u32[]{:S(2)}, u32[]{:S(2)}) async-start(bf16[16,64,128]{2,1,0:T(8,128)(2,1)} %bitcast.6), calls=%async_computation | async-start | bytes 524288 | tf_op jit(solution)/shard_map/all_to_all | solution.py:27
  18.4 3.7 %shard_map.112 = (bf16[2048,128]{1,0:T(8,128)(2,1)S(1)}, bf16[2048,128]{1,0:T(8,128)(2,1)}, bf16[2048,128]{1,0:T(8,128)(2,1)}, bf16[2048,128]{1,0:T(8,128)(2,1)}...) custom-call(s32[4]{0:T(128)S(1)} %pad_add_fusion.at_ref, ...), custom_call_target="tpu_custom_call" | custom-call | tf_op jit(solution)/shard_map/pallas_call | solution.py:46
  22.1 1.9 %collective-permute-start = (bf16[32,64,128]{2,1,0:T(8,128)(2,1)S(1)}, bf16[32,64,128]{2,1,0:T(8,128)(2,1)S(1)}, u32[]{:S(2)}, u32[]{:S(2)}) collective-permute-start(bf16[32,64,128]{2,1,0:T(8,128)(2,1)S(1)} %get-tuple-element.42), channel_id=1, source_target_pairs={{0,1},{1,0},{2,3},{3,2},{4,5},{5,4},{6,7},{7,6},{8,9},{9,8},{10,11... | collective-permute-start | bytes 1572872 | tf_op jit(solution)/shard_map/ppermute | solution.py:23
  24.0 2.4 %collective-permute-start.4 = (bf16[2048,128]{1,0:T(8,128)(2,1)}, bf16[2048,128]{1,0:T(8,128)(2,1)S(1)}, u32[]{:S(2)}, u32[]{:S(2)}) collective-permute-start(bf16[2048,128]{1,0:T(8,128)(2,1)} %get-tuple-element.46), channel_id=1, source_target_pairs={{0,16},{16,32},{32,48},{48,0},{1,17},{17,33},{33,49},{49,1},{2,18}... | collective-permute-start | bytes 1572872 | tf_op jit(solution)/shard_map/ppermute | solution.py:19
  26.4 3.5 %collective-permute-start.5 = (bf16[2048,128]{1,0:T(8,128)(2,1)}, bf16[2048,128]{1,0:T(8,128)(2,1)S(1)}, u32[]{:S(2)}, u32[]{:S(2)}) collective-permute-start(bf16[2048,128]{1,0:T(8,128)(2,1)} %get-tuple-element.47), channel_id=1, source_target_pairs={{0,48},{16,0},{32,16},{48,32},{1,49},{17,1},{33,17},{49,33},{2,50}... | collective-permute-start | bytes 1572872 | tf_op jit(solution)/shard_map/ppermute | solution.py:19
  29.9 3.3 %collective-permute-start.6 = (bf16[2048,128]{1,0:T(8,128)(2,1)}, bf16[2048,128]{1,0:T(8,128)(2,1)S(1)}, u32[]{:S(2)}, u32[]{:S(2)}) collective-permute-start(bf16[2048,128]{1,0:T(8,128)(2,1)} %get-tuple-element.48), channel_id=1, source_target_pairs={{0,32},{16,48},{32,0},{48,16},{1,33},{17,49},{33,1},{49,17},{2,34}... | collective-permute-start | bytes 1572872 | tf_op jit(solution)/shard_map/ppermute | solution.py:19
  33.2 3.8 %collective-permute-start.7 = (bf16[192,512]{1,0:T(8,128)(2,1)S(1)}, bf16[192,512]{1,0:T(8,128)(2,1)S(1)}, u32[]{:S(2)}, u32[]{:S(2)}) collective-permute-start(bf16[192,512]{1,0:T(8,128)(2,1)S(1)} %get-tuple-element.49), channel_id=1, source_target_pairs={{0,64},{64,0},{128,192},{192,128},{256,320},{320,256},{384,448},{4... | collective-permute-start | bytes 589832 | tf_op jit(solution)/shard_map/ppermute | solution.py:23
  37.0 0.0 collective-permute-done.other_ref
  37.0 0.0 all-to-all-done
  37.0 4.9 %collective-permute-start.1 = (bf16[2,512,128]{2,1,0:T(8,128)(2,1)}, bf16[2,512,128]{2,1,0:T(8,128)(2,1)S(1)}, u32[]{:S(2)}, u32[]{:S(2)}) collective-permute-start(bf16[2,512,128]{2,1,0:T(8,128)(2,1)} %bitcast.11), channel_id=1, source_target_pairs={{0,12},{4,0},{8,4},{12,8},{1,13},{5,1},{9,5},{13,9},{2,14},{6,2},{... | collective-permute-start | bytes 786440 | tf_op jit(solution)/shard_map/ppermute | solution.py:19
  41.9 0.0 collective-permute-done.7
  41.9 4.8 %collective-permute-start.2 = (bf16[2,512,128]{2,1,0:T(8,128)(2,1)}, bf16[2,512,128]{2,1,0:T(8,128)(2,1)S(1)}, u32[]{:S(2)}, u32[]{:S(2)}) collective-permute-start(bf16[2,512,128]{2,1,0:T(8,128)(2,1)} %bitcast.11), channel_id=1, source_target_pairs={{0,8},{4,12},{8,0},{12,4},{1,9},{5,13},{9,1},{13,5},{2,10},{6,14},... | collective-permute-start | bytes 786440 | tf_op jit(solution)/shard_map/ppermute | solution.py:19
  46.8 0.0 collective-permute-done.4.w1
  46.8 2.6 %collective-permute-start.3 = (bf16[2,512,128]{2,1,0:T(8,128)(2,1)}, bf16[2,512,128]{2,1,0:T(8,128)(2,1)S(1)}, u32[]{:S(2)}, u32[]{:S(2)}) collective-permute-start(bf16[2,512,128]{2,1,0:T(8,128)(2,1)} %bitcast.11), channel_id=1, source_target_pairs={{0,4},{4,8},{8,12},{12,0},{1,5},{5,9},{9,13},{13,1},{2,6},{6,10},{... | collective-permute-start | bytes 786440 | tf_op jit(solution)/shard_map/ppermute | solution.py:19
  49.4 5.6 %collective-permute-done.5.w2 = bf16[2048,128]{1,0:T(8,128)(2,1)S(1)} collective-permute-done((bf16[2048,128]{1,0:T(8,128)(2,1)}, bf16[2048,128]{1,0:T(8,128)(2,1)S(1)}, u32[]{:S(2)}, u32[]{:S(2)}) %collective-permute-start.5) | collective-permute-done | bytes 524320 | tf_op jit(solution)/shard_map/ppermute | solution.py:19
  55.0 0.0 collective-permute-done.6.w3
  55.0 0.0 collective-permute-done.1
  55.0 0.0 collective-permute-done.2
  55.0 3.7 %collective-permute-done.3 = bf16[2,512,128]{2,1,0:T(8,128)(2,1)S(1)} collective-permute-done((bf16[2,512,128]{2,1,0:T(8,128)(2,1)}, bf16[2,512,128]{2,1,0:T(8,128)(2,1)S(1)}, u32[]{:S(2)}, u32[]{:S(2)}) %collective-permute-start.3) | collective-permute-done | bytes 262176 | tf_op jit(solution)/shard_map/ppermute | solution.py:19
  58.7 1.1 pad_maximum_fusion.own_ref
  59.8 1.9 %collective-permute-start.8 = (bf16[4,2,512,128]{3,2,1,0:T(8,128)(2,1)S(1)}, bf16[4,2,512,128]{3,2,1,0:T(8,128)(2,1)S(1)}, u32[]{:S(2)}, u32[]{:S(2)}) collective-permute-start(bf16[4,2,512,128]{3,2,1,0:T(8,128)(2,1)S(1)} %pad_maximum_fusion.own_ref), channel_id=1, source_target_pairs={{0,1},{1,0},{2,3},{3,2},{4,5},{5,4},{6,7},{7,6},{8,9},{9,8},{10,11... | collective-permute-start | bytes 3145736 | tf_op jit(solution)/shard_map/ppermute | solution.py:23
  61.7 2.6 %collective-permute-done.8.other_ref = bf16[4,2,512,128]{3,2,1,0:T(8,128)(2,1)S(1)} collective-permute-done((bf16[4,2,512,128]{3,2,1,0:T(8,128)(2,1)S(1)}, bf16[4,2,512,128]{3,2,1,0:T(8,128)(2,1)S(1)}, u32[]{:S(2)}, u32[]{:S(2)}) %collective-permute-start.8) | collective-permute-done | bytes 1048608 | tf_op jit(solution)/shard_map/ppermute | solution.py:23
  64.3 4.0 %shard_map.113 = (f32[128,512]{1,0:T(8,128)S(1)}, bf16[4,128,512]{2,1,0:T(8,128)(2,1)}) custom-call(s32[4]{0:T(128)S(1)} %pad_add_fusion.at_ref, bf16[2048,128]{1,0:T(8,128)(2,1)S(1)} %get-tuple-element.50.w0, bf16[2048,128]{1,0:T(8,128)(2,1)S(1)} %collective-permute-done.4.w1, bf16[2048,128]{1,0:T(8,128)(2,1)S(1)} %collective-permute-done.5.w2, ...), custom_call_target="tpu_custom_call" | custom-call | tf_op jit(solution)/shard_map/pallas_call | solution.py:46
  68.3 5.6 %all-to-all-start.1 = ((bf16[4,128,512]{2,1,0:T(8,128)(2,1)}), bf16[4,128,512]{2,1,0:T(8,128)(2,1)S(1)}, u32[]{:S(2)}, u32[]{:S(2)}) async-start(bf16[4,128,512]{2,1,0:T(8,128)(2,1)} %get-tuple-element.62), calls=%async_computation.1 | async-start | bytes 1048576 | tf_op jit(solution)/shard_map/all_to_all | solution.py:27
  73.9 0.1 convert_add_fusion
  74.0 4.3 %collective-permute-start.10 = (bf16[96,512]{1,0:T(8,128)(2,1)S(1)}, bf16[96,512]{1,0:T(8,128)(2,1)S(1)}, u32[]{:S(2)}, u32[]{:S(2)}) collective-permute-start(bf16[96,512]{1,0:T(8,128)(2,1)S(1)} %fusion.4), channel_id=1, source_target_pairs={{0,128},{64,192},{128,0},{192,64},{256,384},{320,448},{384,256},{4... | collective-permute-start | bytes 294920 | tf_op jit(solution)/shard_map/ppermute | solution.py:23
  78.3 3.6 %all-to-all-done.1 = bf16[4,128,512]{2,1,0:T(8,128)(2,1)S(1)} async-done(((bf16[4,128,512]{2,1,0:T(8,128)(2,1)}), bf16[4,128,512]{2,1,0:T(8,128)(2,1)S(1)}, u32[]{:S(2)}, u32[]{:S(2)}) %all-to-all-start.1) | async-done | bytes 524320 | tf_op jit(solution)/shard_map/all_to_all | solution.py:27
  81.9 0.1 bitcast_add_fusion
  82.0 11.9 %collective-permute-start.9 = (bf16[64,512]{1,0:T(8,128)(2,1)S(1)}, bf16[64,512]{1,0:T(8,128)(2,1)S(1)}, u32[]{:S(2)}, u32[]{:S(2)}) collective-permute-start(bf16[64,512]{1,0:T(8,128)(2,1)S(1)} %fusion.1), channel_id=1, source_target_pairs={{0,2},{2,0},{1,3},{3,1},{4,6},{6,4},{5,7},{7,5},{8,10},{10,8},{9,1... | collective-permute-start | bytes 196616 | tf_op jit(solution)/shard_map/ppermute | solution.py:23
  93.9 0.0 collective-permute-done.10
  94.0 3.1 %collective-permute-done.9 = bf16[64,512]{1,0:T(8,128)(2,1)S(1)} collective-permute-done((bf16[64,512]{1,0:T(8,128)(2,1)S(1)}, bf16[64,512]{1,0:T(8,128)(2,1)S(1)}, u32[]{:S(2)}, u32[]{:S(2)}) %collective-permute-start.9) | collective-permute-done | bytes 65568 | tf_op jit(solution)/shard_map/ppermute | solution.py:23
  97.1 0.1 copy.12
  97.2 1.8 %broadcast_in_dim.14 = bf16[16,512,128]{2,1,0:T(8,128)(2,1)} broadcast(bf16[512,128]{1,0:T(8,128)(2,1)S(1)} %copy.12), dimensions={1,2} | broadcast | bytes 2228224 | tf_op jit(solution)/shard_map/broadcast_in_dim | solution.py:32
  99.0 6.5 %all-to-all-start.2 = ((bf16[16,512,128]{2,1,0:T(8,128)(2,1)}), bf16[16,512,128]{2,1,0:T(8,128)(2,1)S(1)}, u32[]{:S(2)}, u32[]{:S(2)}) async-start(bf16[16,512,128]{2,1,0:T(8,128)(2,1)} %broadcast_in_dim.14), calls=%async_computation.2 | async-start | bytes 4194304 | tf_op jit(solution)/shard_map/all_to_all | solution.py:27
  105.5 10.0 %collective-permute-start.11 = (bf16[96,512]{1,0:T(8,128)(2,1)S(1)}, bf16[96,512]{1,0:T(8,128)(2,1)S(1)}, u32[]{:S(2)}, u32[]{:S(2)}) collective-permute-start(bf16[96,512]{1,0:T(8,128)(2,1)S(1)} %fusion), channel_id=1, source_target_pairs={{0,256},{64,320},{128,384},{192,448},{256,0},{320,64},{384,128},{4... | collective-permute-start | bytes 294920 | tf_op jit(solution)/shard_map/ppermute | solution.py:23
  115.5 6.7 %collective-permute-done.11 = bf16[96,512]{1,0:T(8,128)(2,1)S(1)} collective-permute-done((bf16[96,512]{1,0:T(8,128)(2,1)S(1)}, bf16[96,512]{1,0:T(8,128)(2,1)S(1)}, u32[]{:S(2)}, u32[]{:S(2)}) %collective-permute-start.11) | collective-permute-done | bytes 98336 | tf_op jit(solution)/shard_map/ppermute | solution.py:23
  122.3 0.0 copy-start
  122.3 2.9 %collective-permute-start.12 = (bf16[96,512]{1,0:T(8,128)(2,1)S(1)}, bf16[96,512]{1,0:T(8,128)(2,1)S(1)}, u32[]{:S(2)}, u32[]{:S(2)}) collective-permute-start(bf16[96,512]{1,0:T(8,128)(2,1)S(1)} %multiply_convert_fusion), channel_id=1, source_target_pairs={{0,128},{64,192},{128,0},{192,64},{256,384},{320,448},{384,256},{4... | collective-permute-start | bytes 294920 | tf_op jit(solution)/shard_map/ppermute | solution.py:23
  125.2 4.5 %collective-permute-done.12 = bf16[96,512]{1,0:T(8,128)(2,1)S(1)} collective-permute-done((bf16[96,512]{1,0:T(8,128)(2,1)S(1)}, bf16[96,512]{1,0:T(8,128)(2,1)S(1)}, u32[]{:S(2)}, u32[]{:S(2)}) %collective-permute-start.12) | collective-permute-done | bytes 98336 | tf_op jit(solution)/shard_map/ppermute | solution.py:23
  129.7 1.6 all-to-all-done.2.hidden_ref
  131.2 3.0 %shard_map.114 = (f32[512,128]{1,0:T(8,128)S(1)}, f32[512,128]{1,0:T(8,128)}) custom-call(s32[4]{0:T(128)S(1)} %pad_add_fusion.at_ref, bf16[32,2,64,128]{3,2,1,0:T(8,128)(2,1)} %bitcast.58, bf16[32,64,128]{2,1,0:T(8,128)(2,1)S(1)} %collective-permute-done.other_ref, bf16[16,512,128]{2,1,0:T(8,128)(2,1)S(1)} %all-to-all-done.2.hidden_ref), custom_call_target="tpu_custom_call" | custom-call | tf_op jit(solution)/shard_map/pallas_call | solution.py:46
  134.3 1.9 %collective-permute-start.13 = (f32[512,128]{1,0:T(8,128)}, f32[512,128]{1,0:T(8,128)S(1)}, u32[]{:S(2)}, u32[]{:S(2)}) collective-permute-start(f32[512,128]{1,0:T(8,128)} %get-tuple-element.69), channel_id=1, source_target_pairs={{0,1},{1,0},{2,3},{3,2},{4,5},{5,4},{6,7},{7,6},{8,9},{9,8},{10,11... | collective-permute-start | bytes 786440 | tf_op jit(solution)/shard_map/ppermute | solution.py:23
  136.2 1.7 %collective-permute-done.13 = f32[512,128]{1,0:T(8,128)S(1)} collective-permute-done((f32[512,128]{1,0:T(8,128)}, f32[512,128]{1,0:T(8,128)S(1)}, u32[]{:S(2)}, u32[]{:S(2)}) %collective-permute-start.13) | collective-permute-done | bytes 262176 | tf_op jit(solution)/shard_map/ppermute | solution.py:23
  137.9 0.7 add_convert_fusion
  138.6 13.6 %all-to-all-start.3 = ((bf16[8,64,128]{2,1,0:T(8,128)(2,1)}), bf16[8,64,128]{2,1,0:T(8,128)(2,1)S(1)}, u32[]{:S(2)}, u32[]{:S(2)}) async-start(bf16[8,64,128]{2,1,0:T(8,128)(2,1)} %bitcast.26), calls=%async_computation.3 | async-start | bytes 262144 | tf_op jit(solution)/shard_map/all_to_all | solution.py:27
  152.3 3.9 %collective-permute-start.14 = (bf16[2,96,512]{2,1,0:T(8,128)(2,1)S(1)}, bf16[2,96,512]{2,1,0:T(8,128)(2,1)S(1)}, u32[]{:S(2)}, u32[]{:S(2)}) collective-permute-start(bf16[2,96,512]{2,1,0:T(8,128)(2,1)S(1)} %pad_maximum_fusion.2), channel_id=1, source_target_pairs={{0,64},{64,0},{128,192},{192,128},{256,320},{320,256},{384,448},{4... | collective-permute-start | bytes 589832 | tf_op jit(solution)/shard_map/ppermute | solution.py:23
  156.2 0.0 copy-done
  156.2 5.7 %collective-permute-done.14 = bf16[2,96,512]{2,1,0:T(8,128)(2,1)S(1)} collective-permute-done((bf16[2,96,512]{2,1,0:T(8,128)(2,1)S(1)}, bf16[2,96,512]{2,1,0:T(8,128)(2,1)S(1)}, u32[]{:S(2)}, u32[]{:S(2)}) %collective-permute-start.14) | collective-permute-done | bytes 196640 | tf_op jit(solution)/shard_map/ppermute | solution.py:23
  161.9 3.0 %all-to-all-done.3 = bf16[8,64,128]{2,1,0:T(8,128)(2,1)S(1)} async-done(((bf16[8,64,128]{2,1,0:T(8,128)(2,1)}), bf16[8,64,128]{2,1,0:T(8,128)(2,1)S(1)}, u32[]{:S(2)}, u32[]{:S(2)}) %all-to-all-start.3) | async-done | bytes 131104 | tf_op jit(solution)/shard_map/all_to_all | solution.py:27
  165.0 0.9 slice_convert_fusion
  165.8 0.3 fusion.7
  166.1 0.7 fusion.6
  (10 shorter events, 0.3 us)
Async XLA Ops:
  3.1 33.9 %all-to-all-start = ((bf16[16,64,128]{2,1,0:T(8,128)(2,1)}), bf16[16,64,128]{2,1,0:T(8,128)(2,1)}, u32[]{:S(2)}, u32[]{:S(2)}) async-start(bf16[16,64,128]{2,1,0:T(8,128)(2,1)} %bitcast.6), calls=%async_computation | async-start | bytes 524288 | tf_op jit(solution)/shard_map/all_to_all | solution.py:27
  22.1 14.9 %collective-permute-start = (bf16[32,64,128]{2,1,0:T(8,128)(2,1)S(1)}, bf16[32,64,128]{2,1,0:T(8,128)(2,1)S(1)}, u32[]{:S(2)}, u32[]{:S(2)}) collective-permute-start(bf16[32,64,128]{2,1,0:T(8,128)(2,1)S(1)} %get-tuple-element.42), channel_id=1, source_target_pairs={{0,1},{1,0},{2,3},{3,2},{4,5},{5,4},{6,7},{7,6},{8,9},{9,8},{10,11... | collective-permute-start | bytes 1572872 | tf_op jit(solution)/shard_map/ppermute | solution.py:23
  24.0 22.8 %collective-permute-start.4 = (bf16[2048,128]{1,0:T(8,128)(2,1)}, bf16[2048,128]{1,0:T(8,128)(2,1)S(1)}, u32[]{:S(2)}, u32[]{:S(2)}) collective-permute-start(bf16[2048,128]{1,0:T(8,128)(2,1)} %get-tuple-element.46), channel_id=1, source_target_pairs={{0,16},{16,32},{32,48},{48,0},{1,17},{17,33},{33,49},{49,1},{2,18}... | collective-permute-start | bytes 1572872 | tf_op jit(solution)/shard_map/ppermute | solution.py:19
  26.4 28.6 %collective-permute-start.5 = (bf16[2048,128]{1,0:T(8,128)(2,1)}, bf16[2048,128]{1,0:T(8,128)(2,1)S(1)}, u32[]{:S(2)}, u32[]{:S(2)}) collective-permute-start(bf16[2048,128]{1,0:T(8,128)(2,1)} %get-tuple-element.47), channel_id=1, source_target_pairs={{0,48},{16,0},{32,16},{48,32},{1,49},{17,1},{33,17},{49,33},{2,50}... | collective-permute-start | bytes 1572872 | tf_op jit(solution)/shard_map/ppermute | solution.py:19
  29.9 25.1 %collective-permute-start.6 = (bf16[2048,128]{1,0:T(8,128)(2,1)}, bf16[2048,128]{1,0:T(8,128)(2,1)S(1)}, u32[]{:S(2)}, u32[]{:S(2)}) collective-permute-start(bf16[2048,128]{1,0:T(8,128)(2,1)} %get-tuple-element.48), channel_id=1, source_target_pairs={{0,32},{16,48},{32,0},{48,16},{1,33},{17,49},{33,1},{49,17},{2,34}... | collective-permute-start | bytes 1572872 | tf_op jit(solution)/shard_map/ppermute | solution.py:19
  33.2 8.7 %collective-permute-start.7 = (bf16[192,512]{1,0:T(8,128)(2,1)S(1)}, bf16[192,512]{1,0:T(8,128)(2,1)S(1)}, u32[]{:S(2)}, u32[]{:S(2)}) collective-permute-start(bf16[192,512]{1,0:T(8,128)(2,1)S(1)} %get-tuple-element.49), channel_id=1, source_target_pairs={{0,64},{64,0},{128,192},{192,128},{256,320},{320,256},{384,448},{4... | collective-permute-start | bytes 589832 | tf_op jit(solution)/shard_map/ppermute | solution.py:23
  37.0 18.0 %collective-permute-start.1 = (bf16[2,512,128]{2,1,0:T(8,128)(2,1)}, bf16[2,512,128]{2,1,0:T(8,128)(2,1)S(1)}, u32[]{:S(2)}, u32[]{:S(2)}) collective-permute-start(bf16[2,512,128]{2,1,0:T(8,128)(2,1)} %bitcast.11), channel_id=1, source_target_pairs={{0,12},{4,0},{8,4},{12,8},{1,13},{5,1},{9,5},{13,9},{2,14},{6,2},{... | collective-permute-start | bytes 786440 | tf_op jit(solution)/shard_map/ppermute | solution.py:19
  41.9 13.1 %collective-permute-start.2 = (bf16[2,512,128]{2,1,0:T(8,128)(2,1)}, bf16[2,512,128]{2,1,0:T(8,128)(2,1)S(1)}, u32[]{:S(2)}, u32[]{:S(2)}) collective-permute-start(bf16[2,512,128]{2,1,0:T(8,128)(2,1)} %bitcast.11), channel_id=1, source_target_pairs={{0,8},{4,12},{8,0},{12,4},{1,9},{5,13},{9,1},{13,5},{2,10},{6,14},... | collective-permute-start | bytes 786440 | tf_op jit(solution)/shard_map/ppermute | solution.py:19
  46.8 11.9 %collective-permute-start.3 = (bf16[2,512,128]{2,1,0:T(8,128)(2,1)}, bf16[2,512,128]{2,1,0:T(8,128)(2,1)S(1)}, u32[]{:S(2)}, u32[]{:S(2)}) collective-permute-start(bf16[2,512,128]{2,1,0:T(8,128)(2,1)} %bitcast.11), channel_id=1, source_target_pairs={{0,4},{4,8},{8,12},{12,0},{1,5},{5,9},{9,13},{13,1},{2,6},{6,10},{... | collective-permute-start | bytes 786440 | tf_op jit(solution)/shard_map/ppermute | solution.py:19
  59.8 4.6 %collective-permute-start.8 = (bf16[4,2,512,128]{3,2,1,0:T(8,128)(2,1)S(1)}, bf16[4,2,512,128]{3,2,1,0:T(8,128)(2,1)S(1)}, u32[]{:S(2)}, u32[]{:S(2)}) collective-permute-start(bf16[4,2,512,128]{3,2,1,0:T(8,128)(2,1)S(1)} %pad_maximum_fusion.own_ref), channel_id=1, source_target_pairs={{0,1},{1,0},{2,3},{3,2},{4,5},{5,4},{6,7},{7,6},{8,9},{9,8},{10,11... | collective-permute-start | bytes 3145736 | tf_op jit(solution)/shard_map/ppermute | solution.py:23
  68.3 13.5 %all-to-all-start.1 = ((bf16[4,128,512]{2,1,0:T(8,128)(2,1)}), bf16[4,128,512]{2,1,0:T(8,128)(2,1)S(1)}, u32[]{:S(2)}, u32[]{:S(2)}) async-start(bf16[4,128,512]{2,1,0:T(8,128)(2,1)} %get-tuple-element.62), calls=%async_computation.1 | async-start | bytes 1048576 | tf_op jit(solution)/shard_map/all_to_all | solution.py:27
  74.0 20.0 %collective-permute-start.10 = (bf16[96,512]{1,0:T(8,128)(2,1)S(1)}, bf16[96,512]{1,0:T(8,128)(2,1)S(1)}, u32[]{:S(2)}, u32[]{:S(2)}) collective-permute-start(bf16[96,512]{1,0:T(8,128)(2,1)S(1)} %fusion.4), channel_id=1, source_target_pairs={{0,128},{64,192},{128,0},{192,64},{256,384},{320,448},{384,256},{4... | collective-permute-start | bytes 294920 | tf_op jit(solution)/shard_map/ppermute | solution.py:23
  82.0 15.0 %collective-permute-start.9 = (bf16[64,512]{1,0:T(8,128)(2,1)S(1)}, bf16[64,512]{1,0:T(8,128)(2,1)S(1)}, u32[]{:S(2)}, u32[]{:S(2)}) collective-permute-start(bf16[64,512]{1,0:T(8,128)(2,1)S(1)} %fusion.1), channel_id=1, source_target_pairs={{0,2},{2,0},{1,3},{3,1},{4,6},{6,4},{5,7},{7,5},{8,10},{10,8},{9,1... | collective-permute-start | bytes 196616 | tf_op jit(solution)/shard_map/ppermute | solution.py:23
  99.0 32.2 %all-to-all-start.2 = ((bf16[16,512,128]{2,1,0:T(8,128)(2,1)}), bf16[16,512,128]{2,1,0:T(8,128)(2,1)S(1)}, u32[]{:S(2)}, u32[]{:S(2)}) async-start(bf16[16,512,128]{2,1,0:T(8,128)(2,1)} %broadcast_in_dim.14), calls=%async_computation.2 | async-start | bytes 4194304 | tf_op jit(solution)/shard_map/all_to_all | solution.py:27
  105.5 16.7 %collective-permute-start.11 = (bf16[96,512]{1,0:T(8,128)(2,1)S(1)}, bf16[96,512]{1,0:T(8,128)(2,1)S(1)}, u32[]{:S(2)}, u32[]{:S(2)}) collective-permute-start(bf16[96,512]{1,0:T(8,128)(2,1)S(1)} %fusion), channel_id=1, source_target_pairs={{0,256},{64,320},{128,384},{192,448},{256,0},{320,64},{384,128},{4... | collective-permute-start | bytes 294920 | tf_op jit(solution)/shard_map/ppermute | solution.py:23
  122.3 34.0 %copy-start = (f32[128,2]{0,1:T(2,128)S(1)}, f32[128,2]{0,1:T(2,128)}, u32[]{:S(2)}) copy-start(f32[128,2]{0,1:T(2,128)} %param.13) | copy-start | bytes 3076
  122.3 7.4 %collective-permute-start.12 = (bf16[96,512]{1,0:T(8,128)(2,1)S(1)}, bf16[96,512]{1,0:T(8,128)(2,1)S(1)}, u32[]{:S(2)}, u32[]{:S(2)}) collective-permute-start(bf16[96,512]{1,0:T(8,128)(2,1)S(1)} %multiply_convert_fusion), channel_id=1, source_target_pairs={{0,128},{64,192},{128,0},{192,64},{256,384},{320,448},{384,256},{4... | collective-permute-start | bytes 294920 | tf_op jit(solution)/shard_map/ppermute | solution.py:23
  134.3 3.6 %collective-permute-start.13 = (f32[512,128]{1,0:T(8,128)}, f32[512,128]{1,0:T(8,128)S(1)}, u32[]{:S(2)}, u32[]{:S(2)}) collective-permute-start(f32[512,128]{1,0:T(8,128)} %get-tuple-element.69), channel_id=1, source_target_pairs={{0,1},{1,0},{2,3},{3,2},{4,5},{5,4},{6,7},{7,6},{8,9},{9,8},{10,11... | collective-permute-start | bytes 786440 | tf_op jit(solution)/shard_map/ppermute | solution.py:23
  138.6 26.3 %all-to-all-start.3 = ((bf16[8,64,128]{2,1,0:T(8,128)(2,1)}), bf16[8,64,128]{2,1,0:T(8,128)(2,1)S(1)}, u32[]{:S(2)}, u32[]{:S(2)}) async-start(bf16[8,64,128]{2,1,0:T(8,128)(2,1)} %bitcast.26), calls=%async_computation.3 | async-start | bytes 262144 | tf_op jit(solution)/shard_map/all_to_all | solution.py:27
  152.3 9.6 %collective-permute-start.14 = (bf16[2,96,512]{2,1,0:T(8,128)(2,1)S(1)}, bf16[2,96,512]{2,1,0:T(8,128)(2,1)S(1)}, u32[]{:S(2)}, u32[]{:S(2)}) collective-permute-start(bf16[2,96,512]{2,1,0:T(8,128)(2,1)S(1)} %pad_maximum_fusion.2), channel_id=1, source_target_pairs={{0,64},{64,0},{128,192},{192,128},{256,320},{320,256},{384,448},{4... | collective-permute-start | bytes 589832 | tf_op jit(solution)/shard_map/ppermute | solution.py:23

commit v4 on v3

--- a/solution.py
+++ b/solution.py
@@ -245,15 +245,14 @@
         ],
     )
     weights = to_peers(cuts, GATE_ORDER)
-    got = flip(give, "b", 1)
     other_lower = flip(other_lower, "c")
 
-    arrived, other_lower = lax.optimization_barrier((arrived, other_lower))
     rows = arrived.reshape(2, slots, width)
     line = [rows] + [shift(rows, "y", -ahead) for ahead in ROWS_ORDER[1:]]
-    line, weights, got = lax.optimization_barrier((line, weights, got))
+    line, weights, give = lax.optimization_barrier((line, weights, give))
     line = jnp.stack(line)
     line_other = flip(line, "c")
+    got = flip(give, "b", 1)
 
     cols = 2 * hidden_here
     here, others = call(
@@ -275,8 +274,7 @@
     hidden = (jax.nn.silu(gated[:hidden_here]) * gated[hidden_here:]).astype(BF16)
 
     swap = flip(hidden, "zh")
-    slabs = (keep.astype(F32) + got.astype(F32)).astype(BF16)
-    swap, slabs = lax.optimization_barrier((swap, slabs))
+    swap, got = lax.optimization_barrier((swap, got))
 
     both = jnp.where(
         half == 0,
@@ -284,6 +282,7 @@
         jnp.concatenate([swap, hidden], axis=0),
     )
     spread = gather(both.T, ("x", "y"))
+    slabs = (keep.astype(F32) + got.astype(F32)).astype(BF16)
     got = flip(slabs, "b", 4)
     slabs = ((slabs.astype(F32) + got.astype(F32)) / branches).astype(BF16)
     got = flip(slabs, "b", 2)

time: 170 us -> 162 us (0.953); the launches traced: 167 us -> 161 us
  starting transfers between devices: 105 us -> 85.4 us
  waiting for transfers between devices: 41.7 us -> 53.6 us
  other arithmetic: 3.83 us -> 5.62 us
    ppermute x9, waiting for transfers between devices: 24.3 us -> 36.4 us  [flip(): lax.ppermute(array, axis, [(i, i ^ bit) for i in range(lax.axis_size(axis...]
    all_to_all x4, starting transfers between devices: 41 us -> 30.8 us  [exchange(): return lax.all_to_all(blocks, axis, split_axis=0, concat_axis=0, tiled=True)]
    ppermute x9, starting transfers between devices: 42.6 us -> 35.2 us  [flip(): lax.ppermute(array, axis, [(i, i ^ bit) for i in range(lax.axis_size(axis...]
    ppermute x6, starting transfers between devices: 21.5 us -> 19.5 us  [shift(): lax.ppermute(array, axis, [(i, (i + step) % size) for i in range(size)])]
    ppermute x6, waiting for transfers between devices: 9.29 us -> 7.34 us  [shift(): lax.ppermute(array, axis, [(i, (i + step) % size) for i in range(size)])]
    all_to_all x4, waiting for transfers between devices: 8.13 us -> 9.93 us  [exchange(): return lax.all_to_all(blocks, axis, split_axis=0, concat_axis=0, tiled=True)]
  transfers between devices with their start and end apart: 19 -> 19, of which waited for: 11 -> 11; matrix products, arithmetic and copies ran while one was open for 0% -> 1% of each run, Pallas kernels for 2% -> 5%
where the time goes in v4:
time: 162 us; the launch traced here: 161 us
  starting transfers between devices  85.4 us (53%)
  waiting for transfers between devices  53.6 us (33%)
  Pallas kernels  12.4 us (8%)
  other arithmetic  5.62 us (3%)
  local copies, waits for them, and re-layouts  2.56 us (2%)
    ppermute x9, waiting for transfers between devices, flip(): lax.ppermute(array, axis, [(i, i ^ bit) for i in range(lax.axis_size(axis...  36.4 us
    ppermute x9, starting transfers between devices, flip(): lax.ppermute(array, axis, [(i, i ^ bit) for i in range(lax.axis_size(axis...  35.2 us
    all_to_all x4, starting transfers between devices, exchange(): return lax.all_to_all(blocks, axis, split_axis=0, concat_axis=0, tiled=True)  30.8 us
    ppermute x6, starting transfers between devices, shift(): lax.ppermute(array, axis, [(i, (i + step) % size) for i in range(size)])  19.5 us
    pallas_call x4, Pallas kernels, call(): pl.pallas_call(kernel, out_shape=out_shape, in_specs=[pl.BlockSpec(memory...  12.4 us
    all_to_all x4, waiting for transfers between devices, exchange(): return lax.all_to_all(blocks, axis, split_axis=0, concat_axis=0, tiled=True)  9.93 us
    ppermute x6, waiting for transfers between devices, shift(): lax.ppermute(array, axis, [(i, (i + step) % size) for i in range(size)])  7.34 us
  transfers between devices with their start and end apart: 19, of which 11 were waited for; matrix products, arithmetic and copies ran while one was open for 1% of the time, Pallas kernels for 5%

profile of v4, /device:TPU:6, one launch (start us, length us, event | category | flops | bytes accessed | tf_op | source)
XLA Modules:
  0.0 160.9 jit_solution(4369009627437382790)
XLA Ops:
  0.6 0.1 pad_add_fusion.at_ref
  0.7 2.4 %shard_map.112 = (bf16[1024,128]{1,0:T(8,128)(2,1)}, bf16[512,256]{1,0:T(8,128)(2,1)S(1)}) custom-call(s32[4]{0:T(128)S(1)} %pad_add_fusion.at_ref, s32[2,128]{1,0:T(2,128)} %bitcast.70, bf16[128,128]{1,0:T(8,128)(2,1)} %tokens_hbm.1), custom_call_target="tpu_custom_call" | custom-call | tf_op jit(solution)/shard_map/pallas_call | solution.py:46
  3.1 15.3 %all-to-all-start = ((bf16[16,64,128]{2,1,0:T(8,128)(2,1)}), bf16[16,64,128]{2,1,0:T(8,128)(2,1)}, u32[]{:S(2)}, u32[]{:S(2)}) async-start(bf16[16,64,128]{2,1,0:T(8,128)(2,1)} %bitcast.10), calls=%async_computation | async-start | bytes 524288 | tf_op jit(solution)/shard_map/all_to_all | solution.py:27
  18.4 3.7 %shard_map.111 = (bf16[2048,128]{1,0:T(8,128)(2,1)S(1)}, bf16[2048,128]{1,0:T(8,128)(2,1)}, bf16[2048,128]{1,0:T(8,128)(2,1)}, bf16[2048,128]{1,0:T(8,128)(2,1)}...) custom-call(s32[4]{0:T(128)S(1)} %pad_add_fusion.at_ref, ...), custom_call_target="tpu_custom_call" | custom-call | tf_op jit(solution)/shard_map/pallas_call | solution.py:46
  22.1 2.4 %collective-permute-start.4 = (bf16[2048,128]{1,0:T(8,128)(2,1)}, bf16[2048,128]{1,0:T(8,128)(2,1)S(1)}, u32[]{:S(2)}, u32[]{:S(2)}) collective-permute-start(bf16[2048,128]{1,0:T(8,128)(2,1)} %get-tuple-element.42), channel_id=1, source_target_pairs={{0,16},{16,32},{32,48},{48,0},{1,17},{17,33},{33,49},{49,1},{2,18}... | collective-permute-start | bytes 1572872 | tf_op jit(solution)/shard_map/ppermute | solution.py:19
  24.5 3.5 %collective-permute-start.5 = (bf16[2048,128]{1,0:T(8,128)(2,1)}, bf16[2048,128]{1,0:T(8,128)(2,1)S(1)}, u32[]{:S(2)}, u32[]{:S(2)}) collective-permute-start(bf16[2048,128]{1,0:T(8,128)(2,1)} %get-tuple-element.43), channel_id=1, source_target_pairs={{0,48},{16,0},{32,16},{48,32},{1,49},{17,1},{33,17},{49,33},{2,50}... | collective-permute-start | bytes 1572872 | tf_op jit(solution)/shard_map/ppermute | solution.py:19
  27.9 3.3 %collective-permute-start.6 = (bf16[2048,128]{1,0:T(8,128)(2,1)}, bf16[2048,128]{1,0:T(8,128)(2,1)S(1)}, u32[]{:S(2)}, u32[]{:S(2)}) collective-permute-start(bf16[2048,128]{1,0:T(8,128)(2,1)} %get-tuple-element.44), channel_id=1, source_target_pairs={{0,32},{16,48},{32,0},{48,16},{1,33},{17,49},{33,1},{49,17},{2,34}... | collective-permute-start | bytes 1572872 | tf_op jit(solution)/shard_map/ppermute | solution.py:19
  31.3 5.5 %all-to-all-done = bf16[16,64,128]{2,1,0:T(8,128)(2,1)} async-done(((bf16[16,64,128]{2,1,0:T(8,128)(2,1)}), bf16[16,64,128]{2,1,0:T(8,128)(2,1)}, u32[]{:S(2)}, u32[]{:S(2)}) %all-to-all-start) | async-done | bytes 262176 | tf_op jit(solution)/shard_map/all_to_all | solution.py:27
  36.8 4.9 %collective-permute-start.1 = (bf16[2,512,128]{2,1,0:T(8,128)(2,1)}, bf16[2,512,128]{2,1,0:T(8,128)(2,1)S(1)}, u32[]{:S(2)}, u32[]{:S(2)}) collective-permute-start(bf16[2,512,128]{2,1,0:T(8,128)(2,1)} %bitcast.11), channel_id=1, source_target_pairs={{0,12},{4,0},{8,4},{12,8},{1,13},{5,1},{9,5},{13,9},{2,14},{6,2},{... | collective-permute-start | bytes 786440 | tf_op jit(solution)/shard_map/ppermute | solution.py:19
  41.7 2.5 %collective-permute-start.2 = (bf16[2,512,128]{2,1,0:T(8,128)(2,1)}, bf16[2,512,128]{2,1,0:T(8,128)(2,1)S(1)}, u32[]{:S(2)}, u32[]{:S(2)}) collective-permute-start(bf16[2,512,128]{2,1,0:T(8,128)(2,1)} %bitcast.11), channel_id=1, source_target_pairs={{0,8},{4,12},{8,0},{12,4},{1,9},{5,13},{9,1},{13,5},{2,10},{6,14},... | collective-permute-start | bytes 786440 | tf_op jit(solution)/shard_map/ppermute | solution.py:19
  44.2 0.0 collective-permute-done.4.w1
  44.3 2.9 %collective-permute-start.3 = (bf16[2,512,128]{2,1,0:T(8,128)(2,1)}, bf16[2,512,128]{2,1,0:T(8,128)(2,1)S(1)}, u32[]{:S(2)}, u32[]{:S(2)}) collective-permute-start(bf16[2,512,128]{2,1,0:T(8,128)(2,1)} %bitcast.11), channel_id=1, source_target_pairs={{0,4},{4,8},{8,12},{12,0},{1,5},{5,9},{9,13},{13,1},{2,6},{6,10},{... | collective-permute-start | bytes 786440 | tf_op jit(solution)/shard_map/ppermute | solution.py:19
  47.1 5.0 %collective-permute-done.5.w2 = bf16[2048,128]{1,0:T(8,128)(2,1)S(1)} collective-permute-done((bf16[2048,128]{1,0:T(8,128)(2,1)}, bf16[2048,128]{1,0:T(8,128)(2,1)S(1)}, u32[]{:S(2)}, u32[]{:S(2)}) %collective-permute-start.5) | collective-permute-done | bytes 524320 | tf_op jit(solution)/shard_map/ppermute | solution.py:19
  52.1 0.0 collective-permute-done.6.w3
  52.1 0.0 collective-permute-done.1
  52.1 0.0 collective-permute-done.2
  52.2 2.3 %collective-permute-done.3 = bf16[2,512,128]{2,1,0:T(8,128)(2,1)S(1)} collective-permute-done((bf16[2,512,128]{2,1,0:T(8,128)(2,1)}, bf16[2,512,128]{2,1,0:T(8,128)(2,1)S(1)}, u32[]{:S(2)}, u32[]{:S(2)}) %collective-permute-start.3) | collective-permute-done | bytes 262176 | tf_op jit(solution)/shard_map/ppermute | solution.py:19
  54.5 1.1 pad_maximum_fusion.own_ref
  55.6 1.9 %collective-permute-start.7 = (bf16[4,2,512,128]{3,2,1,0:T(8,128)(2,1)S(1)}, bf16[4,2,512,128]{3,2,1,0:T(8,128)(2,1)S(1)}, u32[]{:S(2)}, u32[]{:S(2)}) collective-permute-start(bf16[4,2,512,128]{3,2,1,0:T(8,128)(2,1)S(1)} %pad_maximum_fusion.own_ref), channel_id=1, source_target_pairs={{0,1},{1,0},{2,3},{3,2},{4,5},{5,4},{6,7},{7,6},{8,9},{9,8},{10,11... | collective-permute-start | bytes 3145736 | tf_op jit(solution)/shard_map/ppermute | solution.py:23
  57.5 6.7 %collective-permute-start.8 = (bf16[192,512]{1,0:T(8,128)(2,1)}, bf16[192,512]{1,0:T(8,128)(2,1)S(1)}, u32[]{:S(2)}, u32[]{:S(2)}) collective-permute-start(bf16[192,512]{1,0:T(8,128)(2,1)} %get-tuple-element.57), channel_id=1, source_target_pairs={{0,64},{64,0},{128,192},{192,128},{256,320},{320,256},{384,448},{4... | collective-permute-start | bytes 589832 | tf_op jit(solution)/shard_map/ppermute | solution.py:23
  64.2 0.0 collective-permute-done.7.other_ref
  64.3 4.0 %shard_map.113 = (f32[128,512]{1,0:T(8,128)S(1)}, bf16[4,128,512]{2,1,0:T(8,128)(2,1)}) custom-call(s32[4]{0:T(128)S(1)} %pad_add_fusion.at_ref, bf16[2048,128]{1,0:T(8,128)(2,1)S(1)} %get-tuple-element.46.w0, bf16[2048,128]{1,0:T(8,128)(2,1)S(1)} %collective-permute-done.4.w1, bf16[2048,128]{1,0:T(8,128)(2,1)S(1)} %collective-permute-done.5.w2, ...), custom_call_target="tpu_custom_call" | custom-call | tf_op jit(solution)/shard_map/pallas_call | solution.py:46
  68.3 1.7 %collective-permute-done.8 = bf16[192,512]{1,0:T(8,128)(2,1)S(1)} collective-permute-done((bf16[192,512]{1,0:T(8,128)(2,1)}, bf16[192,512]{1,0:T(8,128)(2,1)S(1)}, u32[]{:S(2)}, u32[]{:S(2)}) %collective-permute-start.8) | collective-permute-done | bytes 196640 | tf_op jit(solution)/shard_map/ppermute | solution.py:23
  70.0 4.8 %all-to-all-start.1 = ((bf16[4,128,512]{2,1,0:T(8,128)(2,1)}), bf16[4,128,512]{2,1,0:T(8,128)(2,1)S(1)}, u32[]{:S(2)}, u32[]{:S(2)}) async-start(bf16[4,128,512]{2,1,0:T(8,128)(2,1)} %get-tuple-element.58), calls=%async_computation.1 | async-start | bytes 1048576 | tf_op jit(solution)/shard_map/all_to_all | solution.py:27
  74.8 0.1 convert_add_fusion
  74.8 0.0 copy-start
  74.9 0.6 copy-done
  75.5 3.8 %collective-permute-start.10 = (bf16[96,512]{1,0:T(8,128)(2,1)S(1)}, bf16[96,512]{1,0:T(8,128)(2,1)S(1)}, u32[]{:S(2)}, u32[]{:S(2)}) collective-permute-start(bf16[96,512]{1,0:T(8,128)(2,1)S(1)} %fusion.3), channel_id=1, source_target_pairs={{0,128},{64,192},{128,0},{192,64},{256,384},{320,448},{384,256},{4... | collective-permute-start | bytes 294920 | tf_op jit(solution)/shard_map/ppermute | solution.py:23
  79.4 2.9 %all-to-all-done.1 = bf16[4,128,512]{2,1,0:T(8,128)(2,1)S(1)} async-done(((bf16[4,128,512]{2,1,0:T(8,128)(2,1)}), bf16[4,128,512]{2,1,0:T(8,128)(2,1)S(1)}, u32[]{:S(2)}, u32[]{:S(2)}) %all-to-all-start.1) | async-done | bytes 524320 | tf_op jit(solution)/shard_map/all_to_all | solution.py:27
  82.3 0.1 bitcast_add_fusion
  82.4 7.6 %collective-permute-start.9 = (bf16[64,512]{1,0:T(8,128)(2,1)S(1)}, bf16[64,512]{1,0:T(8,128)(2,1)S(1)}, u32[]{:S(2)}, u32[]{:S(2)}) collective-permute-start(bf16[64,512]{1,0:T(8,128)(2,1)S(1)} %fusion.1), channel_id=1, source_target_pairs={{0,2},{2,0},{1,3},{3,1},{4,6},{6,4},{5,7},{7,5},{8,10},{10,8},{9,1... | collective-permute-start | bytes 196616 | tf_op jit(solution)/shard_map/ppermute | solution.py:23
  90.0 0.0 collective-permute-done.10
  90.0 9.7 %collective-permute-done.9 = bf16[64,512]{1,0:T(8,128)(2,1)S(1)} collective-permute-done((bf16[64,512]{1,0:T(8,128)(2,1)S(1)}, bf16[64,512]{1,0:T(8,128)(2,1)S(1)}, u32[]{:S(2)}, u32[]{:S(2)}) %collective-permute-start.9) | collective-permute-done | bytes 65568 | tf_op jit(solution)/shard_map/ppermute | solution.py:23
  99.8 0.1 copy.12
  99.9 1.8 %broadcast_in_dim.14 = bf16[16,512,128]{2,1,0:T(8,128)(2,1)} broadcast(bf16[512,128]{1,0:T(8,128)(2,1)S(1)} %copy.12), dimensions={1,2} | broadcast | bytes 2228224 | tf_op jit(solution)/shard_map/broadcast_in_dim | solution.py:32
  101.7 5.6 %all-to-all-start.2 = ((bf16[16,512,128]{2,1,0:T(8,128)(2,1)}), bf16[16,512,128]{2,1,0:T(8,128)(2,1)S(1)}, u32[]{:S(2)}, u32[]{:S(2)}) async-start(bf16[16,512,128]{2,1,0:T(8,128)(2,1)} %broadcast_in_dim.14), calls=%async_computation.2 | async-start | bytes 4194304 | tf_op jit(solution)/shard_map/all_to_all | solution.py:27
  107.3 1.9 %collective-permute-start = (bf16[32,64,128]{2,1,0:T(8,128)(2,1)S(1)}, bf16[32,64,128]{2,1,0:T(8,128)(2,1)S(1)}, u32[]{:S(2)}, u32[]{:S(2)}) collective-permute-start(bf16[32,64,128]{2,1,0:T(8,128)(2,1)S(1)} %get-tuple-element.39), channel_id=1, source_target_pairs={{0,1},{1,0},{2,3},{3,2},{4,5},{5,4},{6,7},{7,6},{8,9},{9,8},{10,11... | collective-permute-start | bytes 1572872 | tf_op jit(solution)/shard_map/ppermute | solution.py:23
  109.2 0.9 fusion
  110.2 5.4 %collective-permute-start.11 = (bf16[96,512]{1,0:T(8,128)(2,1)S(1)}, bf16[96,512]{1,0:T(8,128)(2,1)S(1)}, u32[]{:S(2)}, u32[]{:S(2)}) collective-permute-start(bf16[96,512]{1,0:T(8,128)(2,1)S(1)} %fusion), channel_id=1, source_target_pairs={{0,256},{64,320},{128,384},{192,448},{256,0},{320,64},{384,128},{4... | collective-permute-start | bytes 294920 | tf_op jit(solution)/shard_map/ppermute | solution.py:23
  115.6 11.8 %collective-permute-done.11 = bf16[96,512]{1,0:T(8,128)(2,1)S(1)} collective-permute-done((bf16[96,512]{1,0:T(8,128)(2,1)S(1)}, bf16[96,512]{1,0:T(8,128)(2,1)S(1)}, u32[]{:S(2)}, u32[]{:S(2)}) %collective-permute-start.11) | collective-permute-done | bytes 98336 | tf_op jit(solution)/shard_map/ppermute | solution.py:23
  127.5 0.0 copy-start.1
  127.5 1.9 %collective-permute-start.12 = (bf16[96,512]{1,0:T(8,128)(2,1)S(1)}, bf16[96,512]{1,0:T(8,128)(2,1)}, u32[]{:S(2)}, u32[]{:S(2)}) collective-permute-start(bf16[96,512]{1,0:T(8,128)(2,1)S(1)} %multiply_convert_fusion), channel_id=1, source_target_pairs={{0,128},{64,192},{128,0},{192,64},{256,384},{320,448},{384,256},{4... | collective-permute-start | bytes 294920 | tf_op jit(solution)/shard_map/ppermute | solution.py:23
  129.5 5.7 %collective-permute-done.12 = bf16[96,512]{1,0:T(8,128)(2,1)} collective-permute-done((bf16[96,512]{1,0:T(8,128)(2,1)S(1)}, bf16[96,512]{1,0:T(8,128)(2,1)}, u32[]{:S(2)}, u32[]{:S(2)}) %collective-permute-start.12) | collective-permute-done | bytes 98336 | tf_op jit(solution)/shard_map/ppermute | solution.py:23
  135.2 0.0 all-to-all-done.2.hidden_ref
  135.2 0.0 collective-permute-done.other_ref
  135.2 2.3 %shard_map.114 = (f32[512,128]{1,0:T(8,128)S(1)}, f32[512,128]{1,0:T(8,128)S(1)}) custom-call(s32[4]{0:T(128)S(1)} %pad_add_fusion.at_ref, bf16[32,2,64,128]{3,2,1,0:T(8,128)(2,1)} %bitcast.58, bf16[32,64,128]{2,1,0:T(8,128)(2,1)S(1)} %collective-permute-done.other_ref, bf16[16,512,128]{2,1,0:T(8,128)(2,1)S(1)} %all-to-all-done.2.hidden_ref), custom_call_target="tpu_custom_call" | custom-call | tf_op jit(solution)/shard_map/pallas_call | solution.py:46
  137.5 1.9 %collective-permute-start.13 = (f32[512,128]{1,0:T(8,128)S(1)}, f32[512,128]{1,0:T(8,128)S(1)}, u32[]{:S(2)}, u32[]{:S(2)}) collective-permute-start(f32[512,128]{1,0:T(8,128)S(1)} %get-tuple-element.65), channel_id=1, source_target_pairs={{0,1},{1,0},{2,3},{3,2},{4,5},{5,4},{6,7},{7,6},{8,9},{9,8},{10,11... | collective-permute-start | bytes 786440 | tf_op jit(solution)/shard_map/ppermute | solution.py:23
  139.5 1.5 collective-permute-done.13
  140.9 0.7 add_convert_fusion
  141.6 5.1 %all-to-all-start.3 = ((bf16[8,64,128]{2,1,0:T(8,128)(2,1)}), bf16[8,64,128]{2,1,0:T(8,128)(2,1)S(1)}, u32[]{:S(2)}, u32[]{:S(2)}) async-start(bf16[8,64,128]{2,1,0:T(8,128)(2,1)} %bitcast.26), calls=%async_computation.3 | async-start | bytes 262144 | tf_op jit(solution)/shard_map/all_to_all | solution.py:27
  146.7 0.9 select_bitcast_fusion.3
  147.7 3.9 %collective-permute-start.14 = (bf16[2,96,512]{2,1,0:T(8,128)(2,1)S(1)}, bf16[2,96,512]{2,1,0:T(8,128)(2,1)S(1)}, u32[]{:S(2)}, u32[]{:S(2)}) collective-permute-start(bf16[2,96,512]{2,1,0:T(8,128)(2,1)S(1)} %pad_maximum_fusion.2), channel_id=1, source_target_pairs={{0,64},{64,0},{128,192},{192,128},{256,320},{320,256},{384,448},{4... | collective-permute-start | bytes 589832 | tf_op jit(solution)/shard_map/ppermute | solution.py:23
  151.6 0.0 copy-done.1
  151.6 5.8 %collective-permute-done.14 = bf16[2,96,512]{2,1,0:T(8,128)(2,1)S(1)} collective-permute-done((bf16[2,96,512]{2,1,0:T(8,128)(2,1)S(1)}, bf16[2,96,512]{2,1,0:T(8,128)(2,1)S(1)}, u32[]{:S(2)}, u32[]{:S(2)}) %collective-permute-start.14) | collective-permute-done | bytes 196640 | tf_op jit(solution)/shard_map/ppermute | solution.py:23
  157.5 1.5 all-to-all-done.3
  159.1 0.9 slice_convert_fusion
  159.9 0.3 fusion.7
  160.2 0.7 fusion.6
  (8 shorter events, 0.2 us)
Async XLA Ops:
  3.1 33.7 %all-to-all-start = ((bf16[16,64,128]{2,1,0:T(8,128)(2,1)}), bf16[16,64,128]{2,1,0:T(8,128)(2,1)}, u32[]{:S(2)}, u32[]{:S(2)}) async-start(bf16[16,64,128]{2,1,0:T(8,128)(2,1)} %bitcast.10), calls=%async_computation | async-start | bytes 524288 | tf_op jit(solution)/shard_map/all_to_all | solution.py:27
  22.1 22.2 %collective-permute-start.4 = (bf16[2048,128]{1,0:T(8,128)(2,1)}, bf16[2048,128]{1,0:T(8,128)(2,1)S(1)}, u32[]{:S(2)}, u32[]{:S(2)}) collective-permute-start(bf16[2048,128]{1,0:T(8,128)(2,1)} %get-tuple-element.42), channel_id=1, source_target_pairs={{0,16},{16,32},{32,48},{48,0},{1,17},{17,33},{33,49},{49,1},{2,18}... | collective-permute-start | bytes 1572872 | tf_op jit(solution)/shard_map/ppermute | solution.py:19
  24.5 27.7 %collective-permute-start.5 = (bf16[2048,128]{1,0:T(8,128)(2,1)}, bf16[2048,128]{1,0:T(8,128)(2,1)S(1)}, u32[]{:S(2)}, u32[]{:S(2)}) collective-permute-start(bf16[2048,128]{1,0:T(8,128)(2,1)} %get-tuple-element.43), channel_id=1, source_target_pairs={{0,48},{16,0},{32,16},{48,32},{1,49},{17,1},{33,17},{49,33},{2,50}... | collective-permute-start | bytes 1572872 | tf_op jit(solution)/shard_map/ppermute | solution.py:19
  27.9 24.2 %collective-permute-start.6 = (bf16[2048,128]{1,0:T(8,128)(2,1)}, bf16[2048,128]{1,0:T(8,128)(2,1)S(1)}, u32[]{:S(2)}, u32[]{:S(2)}) collective-permute-start(bf16[2048,128]{1,0:T(8,128)(2,1)} %get-tuple-element.44), channel_id=1, source_target_pairs={{0,32},{16,48},{32,0},{48,16},{1,33},{17,49},{33,1},{49,17},{2,34}... | collective-permute-start | bytes 1572872 | tf_op jit(solution)/shard_map/ppermute | solution.py:19
  36.8 15.4 %collective-permute-start.1 = (bf16[2,512,128]{2,1,0:T(8,128)(2,1)}, bf16[2,512,128]{2,1,0:T(8,128)(2,1)S(1)}, u32[]{:S(2)}, u32[]{:S(2)}) collective-permute-start(bf16[2,512,128]{2,1,0:T(8,128)(2,1)} %bitcast.11), channel_id=1, source_target_pairs={{0,12},{4,0},{8,4},{12,8},{1,13},{5,1},{9,5},{13,9},{2,14},{6,2},{... | collective-permute-start | bytes 786440 | tf_op jit(solution)/shard_map/ppermute | solution.py:19
  41.7 10.5 %collective-permute-start.2 = (bf16[2,512,128]{2,1,0:T(8,128)(2,1)}, bf16[2,512,128]{2,1,0:T(8,128)(2,1)S(1)}, u32[]{:S(2)}, u32[]{:S(2)}) collective-permute-start(bf16[2,512,128]{2,1,0:T(8,128)(2,1)} %bitcast.11), channel_id=1, source_target_pairs={{0,8},{4,12},{8,0},{12,4},{1,9},{5,13},{9,1},{13,5},{2,10},{6,14},... | collective-permute-start | bytes 786440 | tf_op jit(solution)/shard_map/ppermute | solution.py:19
  44.3 10.2 %collective-permute-start.3 = (bf16[2,512,128]{2,1,0:T(8,128)(2,1)}, bf16[2,512,128]{2,1,0:T(8,128)(2,1)S(1)}, u32[]{:S(2)}, u32[]{:S(2)}) collective-permute-start(bf16[2,512,128]{2,1,0:T(8,128)(2,1)} %bitcast.11), channel_id=1, source_target_pairs={{0,4},{4,8},{8,12},{12,0},{1,5},{5,9},{9,13},{13,1},{2,6},{6,10},{... | collective-permute-start | bytes 786440 | tf_op jit(solution)/shard_map/ppermute | solution.py:19
  55.6 8.7 %collective-permute-start.7 = (bf16[4,2,512,128]{3,2,1,0:T(8,128)(2,1)S(1)}, bf16[4,2,512,128]{3,2,1,0:T(8,128)(2,1)S(1)}, u32[]{:S(2)}, u32[]{:S(2)}) collective-permute-start(bf16[4,2,512,128]{3,2,1,0:T(8,128)(2,1)S(1)} %pad_maximum_fusion.own_ref), channel_id=1, source_target_pairs={{0,1},{1,0},{2,3},{3,2},{4,5},{5,4},{6,7},{7,6},{8,9},{9,8},{10,11... | collective-permute-start | bytes 3145736 | tf_op jit(solution)/shard_map/ppermute | solution.py:23
  57.5 12.5 %collective-permute-start.8 = (bf16[192,512]{1,0:T(8,128)(2,1)}, bf16[192,512]{1,0:T(8,128)(2,1)S(1)}, u32[]{:S(2)}, u32[]{:S(2)}) collective-permute-start(bf16[192,512]{1,0:T(8,128)(2,1)} %get-tuple-element.57), channel_id=1, source_target_pairs={{0,64},{64,0},{128,192},{192,128},{256,320},{320,256},{384,448},{4... | collective-permute-start | bytes 589832 | tf_op jit(solution)/shard_map/ppermute | solution.py:23
  70.0 12.3 %all-to-all-start.1 = ((bf16[4,128,512]{2,1,0:T(8,128)(2,1)}), bf16[4,128,512]{2,1,0:T(8,128)(2,1)S(1)}, u32[]{:S(2)}, u32[]{:S(2)}) async-start(bf16[4,128,512]{2,1,0:T(8,128)(2,1)} %get-tuple-element.58), calls=%async_computation.1 | async-start | bytes 1048576 | tf_op jit(solution)/shard_map/all_to_all | solution.py:27
  74.8 0.7 copy-start
  75.5 14.5 %collective-permute-start.10 = (bf16[96,512]{1,0:T(8,128)(2,1)S(1)}, bf16[96,512]{1,0:T(8,128)(2,1)S(1)}, u32[]{:S(2)}, u32[]{:S(2)}) collective-permute-start(bf16[96,512]{1,0:T(8,128)(2,1)S(1)} %fusion.3), channel_id=1, source_target_pairs={{0,128},{64,192},{128,0},{192,64},{256,384},{320,448},{384,256},{4... | collective-permute-start | bytes 294920 | tf_op jit(solution)/shard_map/ppermute | solution.py:23
  82.4 17.3 %collective-permute-start.9 = (bf16[64,512]{1,0:T(8,128)(2,1)S(1)}, bf16[64,512]{1,0:T(8,128)(2,1)S(1)}, u32[]{:S(2)}, u32[]{:S(2)}) collective-permute-start(bf16[64,512]{1,0:T(8,128)(2,1)S(1)} %fusion.1), channel_id=1, source_target_pairs={{0,2},{2,0},{1,3},{3,1},{4,6},{6,4},{5,7},{7,5},{8,10},{10,8},{9,1... | collective-permute-start | bytes 196616 | tf_op jit(solution)/shard_map/ppermute | solution.py:23
  101.7 33.5 %all-to-all-start.2 = ((bf16[16,512,128]{2,1,0:T(8,128)(2,1)}), bf16[16,512,128]{2,1,0:T(8,128)(2,1)S(1)}, u32[]{:S(2)}, u32[]{:S(2)}) async-start(bf16[16,512,128]{2,1,0:T(8,128)(2,1)} %broadcast_in_dim.14), calls=%async_computation.2 | async-start | bytes 4194304 | tf_op jit(solution)/shard_map/all_to_all | solution.py:27
  107.3 27.9 %collective-permute-start = (bf16[32,64,128]{2,1,0:T(8,128)(2,1)S(1)}, bf16[32,64,128]{2,1,0:T(8,128)(2,1)S(1)}, u32[]{:S(2)}, u32[]{:S(2)}) collective-permute-start(bf16[32,64,128]{2,1,0:T(8,128)(2,1)S(1)} %get-tuple-element.39), channel_id=1, source_target_pairs={{0,1},{1,0},{2,3},{3,2},{4,5},{5,4},{6,7},{7,6},{8,9},{9,8},{10,11... | collective-permute-start | bytes 1572872 | tf_op jit(solution)/shard_map/ppermute | solution.py:23
  110.2 17.3 %collective-permute-start.11 = (bf16[96,512]{1,0:T(8,128)(2,1)S(1)}, bf16[96,512]{1,0:T(8,128)(2,1)S(1)}, u32[]{:S(2)}, u32[]{:S(2)}) collective-permute-start(bf16[96,512]{1,0:T(8,128)(2,1)S(1)} %fusion), channel_id=1, source_target_pairs={{0,256},{64,320},{128,384},{192,448},{256,0},{320,64},{384,128},{4... | collective-permute-start | bytes 294920 | tf_op jit(solution)/shard_map/ppermute | solution.py:23
  127.5 24.1 %copy-start.1 = (f32[128,2]{0,1:T(2,128)S(1)}, f32[128,2]{0,1:T(2,128)}, u32[]{:S(2)}) copy-start(f32[128,2]{0,1:T(2,128)} %param.13) | copy-start | bytes 3076
  127.5 7.7 %collective-permute-start.12 = (bf16[96,512]{1,0:T(8,128)(2,1)S(1)}, bf16[96,512]{1,0:T(8,128)(2,1)}, u32[]{:S(2)}, u32[]{:S(2)}) collective-permute-start(bf16[96,512]{1,0:T(8,128)(2,1)S(1)} %multiply_convert_fusion), channel_id=1, source_target_pairs={{0,128},{64,192},{128,0},{192,64},{256,384},{320,448},{384,256},{4... | collective-permute-start | bytes 294920 | tf_op jit(solution)/shard_map/ppermute | solution.py:23
  137.5 3.4 %collective-permute-start.13 = (f32[512,128]{1,0:T(8,128)S(1)}, f32[512,128]{1,0:T(8,128)S(1)}, u32[]{:S(2)}, u32[]{:S(2)}) collective-permute-start(f32[512,128]{1,0:T(8,128)S(1)} %get-tuple-element.65), channel_id=1, source_target_pairs={{0,1},{1,0},{2,3},{3,2},{4,5},{5,4},{6,7},{7,6},{8,9},{9,8},{10,11... | collective-permute-start | bytes 786440 | tf_op jit(solution)/shard_map/ppermute | solution.py:23
  141.6 17.4 %all-to-all-start.3 = ((bf16[8,64,128]{2,1,0:T(8,128)(2,1)}), bf16[8,64,128]{2,1,0:T(8,128)(2,1)S(1)}, u32[]{:S(2)}, u32[]{:S(2)}) async-start(bf16[8,64,128]{2,1,0:T(8,128)(2,1)} %bitcast.26), calls=%async_computation.3 | async-start | bytes 262144 | tf_op jit(solution)/shard_map/all_to_all | solution.py:27
  147.7 9.8 %collective-permute-start.14 = (bf16[2,96,512]{2,1,0:T(8,128)(2,1)S(1)}, bf16[2,96,512]{2,1,0:T(8,128)(2,1)S(1)}, u32[]{:S(2)}, u32[]{:S(2)}) collective-permute-start(bf16[2,96,512]{2,1,0:T(8,128)(2,1)S(1)} %pad_maximum_fusion.2), channel_id=1, source_target_pairs={{0,64},{64,0},{128,192},{192,128},{256,320},{320,256},{384,448},{4... | collective-permute-start | bytes 589832 | tf_op jit(solution)/shard_map/ppermute | solution.py:23
